TPU v7x, 32 devices: a whole 2x2x4 slice. The times are simulated.
32 devices in a mesh: inner: 16 (over z, y, core), outer: 2 (over x).
Axes of the slice: x: 2, y: 2, z: 4, core: 2. Of those that a mesh axis runs over, the one named last changes fastest.
Arguments:
- samples: float32 [2, 32, 262144], P(None, ('inner', 'outer')), may hold values from -6 to 6
- gram_index: int32 [1048576], P(('inner', 'outer')), may hold values from 0 to 7, as said below
- gram_offset: int32 [1048576], P(('inner', 'outer')), may hold values from 0 to 31
Outputs:
- z_field: float32 [8388608], P(('inner', 'outer'))
- gram_values: float32 [1048576], P(('inner', 'outer'))
Inputs may be any that keep to these rules, and one draw needn't show every extreme that they name: `gram_index`: A device's first Gram point has 0 and its last 7.
All inputs are finite; a program needn't handle non-finite values.
Results may differ from a plain program's by a relative error of at most 0.00007.
Values sent between devices are 32-bit elements; how exact they have to be, the bound alone decides.
A program may use at most 256 MiB of HBM per device.

v0:
```python
import functools
import math

import jax
import jax.numpy as jnp
import numpy as np
from jax import lax
from jax.experimental import pallas as pl
from jax.experimental.pallas import tpu as pltpu
from jax.sharding import PartitionSpec as P

GAP = 8
HALF = 16
UPS = 32
LANES = 128
RADIX = 8
STEPS = 256
TAU = 2.0 * math.pi
RATE = 4.0
MESH = pl.DeviceIdType.MESH
NT = (((1,), (1,)), ((), ()))


def halves(x):
    high = x.astype(jnp.bfloat16)
    low = (x - high.astype(jnp.float32)).astype(jnp.bfloat16)
    return high, low


def np_halves(x):
    x = x.astype(np.float32)
    high = x.astype(jnp.bfloat16)
    low = (x - high.astype(np.float32)).astype(jnp.bfloat16)
    return high, low


def stage_table():
    p = np.arange(RADIX)[:, None, None]
    f = np.arange(STEPS)[None, :, None]
    t = np.arange(STEPS)[None, None, :]
    order = RADIX * STEPS
    angle = (t * (RADIX * f + p) % order) * (-TAU / order)
    return np.stack([*np_halves(np.cos(angle)), *np_halves(np.sin(angle))], axis=1)


def order_table():
    size = GAP * LANES
    p, l = np.divmod(np.arange(size), LANES)
    table = np.zeros((size, size), np.float32)
    table[np.arange(size), GAP * l + p] = 1.0
    return table.astype(jnp.bfloat16)


def weight_table():
    tap = np.arange(1 - HALF, HALF + 1)[:, None]
    distance = np.arange(LANES)[None, :] % UPS / UPS - tap
    spread = HALF / 2.0
    table = np.sinc(distance) * np.exp(-distance * distance / (2.0 * spread * spread))
    return np.broadcast_to(table.astype(np.float32)[:, None, :], (2 * HALF, 8, LANES)).copy()


def radix_8(parts):
    def add(u, v):
        return u[0] + v[0], u[1] + v[1]

    def sub(u, v):
        return u[0] - v[0], u[1] - v[1]

    def turn(u):
        return u[1], -u[0]

    def four(a, b, c, d):
        s, t, u, v = add(a, c), sub(a, c), add(b, d), turn(sub(b, d))
        return add(s, u), add(t, v), sub(s, u), sub(t, v)

    even = four(parts[0], parts[2], parts[4], parts[6])
    odd = four(parts[1], parts[3], parts[5], parts[7])
    r = math.sqrt(0.5)
    odd = (
        odd[0],
        ((odd[1][0] + odd[1][1]) * r, (odd[1][1] - odd[1][0]) * r),
        turn(odd[2]),
        ((odd[3][1] - odd[3][0]) * r, -(odd[3][0] + odd[3][1]) * r),
    )
    return [add(e, o) for e, o in zip(even, odd)] + [sub(e, o) for e, o in zip(even, odd)]


def transform(values):
    size = len(values)
    if size == 1:
        return values
    even, odd = transform(values[0::2]), transform(values[1::2])
    first, second = [], []
    for k in range(size // 2):
        (er, ei), (br, bi) = even[k], odd[k]
        if k == 0:
            tr, ti = br, bi
        elif 4 * k == size:
            tr, ti = bi, -br
        else:
            c, s = math.cos(TAU * k / size), -math.sin(TAU * k / size)
            tr, ti = br * c - bi * s, br * s + bi * c
        first.append((er + tr, ei + ti))
        second.append((er - tr, ei - ti))
    return first + second


def real_transform(values):
    size = len(values)
    even, odd = transform(values[0::2]), transform(values[1::2])
    first, second = [], []
    for k in range(size // 2):
        c, s = math.cos(TAU * k / size), -math.sin(TAU * k / size)
        t = odd[k][0] if k == 0 else odd[k][1] if 4 * k == size else odd[k][0] * c - odd[k][1] * s
        first.append(even[k][0] + t)
        second.append(even[k][0] - t)
    return first + second


def across_kernel(
    inner, outer, x_ref, stage_ref, u_ref, v_ref, last_ref, out_ref, halo_ref,
    parts, rows, send_a, recv_a, send_b, edge, sem_sa, sem_ra, sem_sb, sem_rb, sem_se, sem_re,
):
    devices = inner * outer
    me = lax.axis_index("inner") * outer + lax.axis_index("outer")
    depth = send_a.shape[3]

    def where(device):
        return (device // outer, device % outer)

    def other(step):
        return (me + step) % devices

    barrier = pltpu.get_barrier_semaphore()

    @pl.loop(1, devices)
    def _(step):
        pl.semaphore_signal(barrier, inc=1, device_id=where(other(step)), device_id_type=MESH)

    @pl.loop(0, STEPS // 32)
    def _(tile):
        at = pl.ds(pl.multiple_of(tile * 32, 32), 32)
        done = radix_8([(x_ref[0, q, at], x_ref[1, q, at]) for q in range(RADIX)])
        for p in range(RADIX):
            parts[p, at, :LANES] = done[p][0]
            parts[p, at, LANES:] = done[p][1]

    def dot(a, b):
        return jnp.dot(a, b, preferred_element_type=jnp.float32)

    def dot_nt(a, b):
        return lax.dot_general(a, b, NT, preferred_element_type=jnp.float32)

    last_high, last_low = halves(last_ref[...])

    @pl.loop(0, RADIX)
    def _(p):
        high, low = halves(parts[p])
        cos_high, cos_low, sin_high, sin_low = (stage_ref[p, i] for i in range(4))
        by_cos = dot(cos_high, high) + dot(cos_high, low) + dot(cos_low, high)
        by_sin = dot(sin_high, high) + dot(sin_high, low) + dot(sin_low, high)
        real = by_cos[:, :LANES] - by_sin[:, LANES:]
        imag = by_cos[:, LANES:] + by_sin[:, :LANES]
        vr, vi = v_ref[0, pl.ds(p, 1)], v_ref[1, pl.ds(p, 1)]
        ur, ui = u_ref[0], u_ref[1]
        tr, ti = ur * vr - ui * vi, ur * vi + ui * vr
        both = jnp.concatenate([real * tr - imag * ti, real * ti + imag * tr], axis=1)
        high, low = halves(both)
        z = dot_nt(last_high, high) + dot_nt(last_high, low) + dot_nt(last_low, high)
        for part in range(2):
            block = z[part * LANES : (part + 1) * LANES]
            for side in range(2):
                rows[part, pl.ds(side, LANES, stride=2), :] = block[:, side * LANES : (side + 1) * LANES]
            send_a[:, part, p] = rows[part].reshape(devices, depth, LANES)

    pl.semaphore_wait(barrier, devices - 1)

    def copy_a(target, source):
        return pltpu.make_async_remote_copy(
            src_ref=send_a.at[target], dst_ref=recv_a.at[me],
            send_sem=sem_sa.at[target], recv_sem=sem_ra.at[source],
            device_id=where(target), device_id_type=MESH,
        )

    def copy_b(target, source):
        return pltpu.make_async_remote_copy(
            src_ref=send_b.at[target], dst_ref=out_ref.at[me],
            send_sem=sem_sb.at[target], recv_sem=sem_rb.at[source],
            device_id=where(target), device_id_type=MESH,
        )

    def copy_edge(target, side):
        shift = 1 if side else -1
        return pltpu.make_async_remote_copy(
            src_ref=edge.at[target + shift], dst_ref=halo_ref.at[side],
            send_sem=sem_se.at[target], recv_sem=sem_re.at[side],
            device_id=where(target), device_id_type=MESH,
        )

    @pl.loop(1, devices)
    def _(step):
        copy_a(other(step), me).start()

    recv_a[me] = send_a[me]

    @pl.loop(1, devices)
    def _(step):
        source = other(devices - step)
        copy_a(source, source).wait_recv()

    @pl.loop(0, RADIX)
    def _(p):
        values = [(recv_a[a, 0, p], recv_a[a, 1, p]) for a in range(devices)]
        done = real_transform(values)
        for k in range(devices):
            send_b[k, p] = done[k]

    def fill_edge(row):
        @pl.loop(0, devices)
        def _(k):
            edge[k] = send_b[k, :, row]

    @pl.when(me == 0)
    def _():
        fill_edge(0)

        @pl.loop(1, devices - 1)
        def _(target):
            copy_edge(target, 1).start()

    @pl.when(me == devices - 1)
    def _():
        fill_edge(depth - 1)

        @pl.loop(1, devices - 1)
        def _(target):
            copy_edge(target, 0).start()

    @pl.loop(1, devices)
    def _(step):
        copy_b(other(step), me).start()

    out_ref[me] = send_b[me]

    @pl.when(me == 0)
    def _():
        halo_ref[0] = jnp.zeros(halo_ref.shape[1:], jnp.float32)
        halo_ref[1] = edge[1]

    @pl.when(me == devices - 1)
    def _():
        halo_ref[0] = edge[devices - 2]
        halo_ref[1] = jnp.zeros(halo_ref.shape[1:], jnp.float32)

    @pl.loop(1, devices)
    def _(step):
        source = other(devices - step)
        copy_b(source, source).wait_recv()

    @pl.when(jnp.logical_and(me > 0, me < devices - 1))
    def _():
        copy_edge(me, 0).wait_recv()
        copy_edge(me, 1).wait_recv()

    @pl.when(jnp.logical_or(me == 0, me == devices - 1))
    def _():
        @pl.loop(1, devices - 1)
        def _(target):
            copy_edge(target, 0).wait_send()

    @pl.loop(1, devices)
    def _(step):
        copy_a(other(step), me).wait_send()
        copy_b(other(step), me).wait_send()


def across(samples, inner, outer):
    devices = inner * outer
    seg = samples.shape[2]
    length = seg * devices
    me = lax.axis_index("inner") * outer + lax.axis_index("outer")
    depth = seg // (devices * RADIX * LANES)
    x = samples.reshape(2, RADIX, STEPS, LANES)

    def phase(number, order):
        angle = number.astype(jnp.float32) * (-TAU / order)
        return jnp.cos(angle), jnp.sin(angle)

    f = lax.broadcasted_iota(jnp.int32, (STEPS, LANES), 0)
    u = jnp.stack(phase(f * (lax.broadcasted_iota(jnp.int32, (STEPS, LANES), 1) * devices + me), length // RADIX))
    p = lax.broadcasted_iota(jnp.int32, (RADIX, LANES), 0)
    v = jnp.stack(phase(p * (lax.broadcasted_iota(jnp.int32, (RADIX, LANES), 1) * devices + me), length))
    g = lax.broadcasted_iota(jnp.int32, (LANES, LANES), 0)
    order = LANES * devices
    number = g * (lax.broadcasted_iota(jnp.int32, (LANES, LANES), 1) * devices + me) % order
    cosine, sine = phase(number, order)
    last = jnp.concatenate(
        [jnp.concatenate([cosine, -sine], axis=1), jnp.concatenate([sine, cosine], axis=1)], axis=0
    )
    vmem = pl.BlockSpec(memory_space=pltpu.VMEM)
    block = (devices, RADIX, depth, LANES)
    return pl.pallas_call(
        functools.partial(across_kernel, inner, outer),
        out_shape=(
            jax.ShapeDtypeStruct(block, jnp.float32),
            jax.ShapeDtypeStruct((2, RADIX, LANES), jnp.float32),
        ),
        in_specs=[vmem] * 5,
        out_specs=(vmem, vmem),
        scratch_shapes=[
            pltpu.VMEM((RADIX, STEPS, 2 * LANES), jnp.float32),
            pltpu.VMEM((2, STEPS, LANES), jnp.float32),
            pltpu.VMEM((devices, 2, RADIX, depth, LANES), jnp.float32),
            pltpu.VMEM((devices, 2, RADIX, depth, LANES), jnp.float32),
            pltpu.VMEM(block, jnp.float32),
            pltpu.VMEM((devices, RADIX, LANES), jnp.float32),
        ]
        + [pltpu.SemaphoreType.DMA((devices,))] * 5
        + [pltpu.SemaphoreType.DMA((2,))],
        compiler_params=pltpu.CompilerParams(
            collective_id=0, has_side_effects=True, vmem_limit_bytes=48 * 2**20
        ),
    )(x, jnp.asarray(stage_table()), u, v, last)


def gram_kernel(inner, outer, real_ref, halo_ref, index_ref, offset_ref, weight_ref, order_ref, z_ref, gram_ref, field):
    devices = inner * outer
    depth = real_ref.shape[2]
    seg = STEPS * LANES * GAP
    length = seg * devices
    me = lax.axis_index("inner") * outer + lax.axis_index("outer")
    base = me.astype(jnp.float32) / devices - 0.5

    def scale(first_row, shape):
        row = lax.broadcasted_iota(jnp.int32, shape, 1) + first_row
        at = (row * LANES + lax.broadcasted_iota(jnp.int32, shape, 2)) * GAP + lax.broadcasted_iota(jnp.int32, shape, 0)
        centred = base + at.astype(jnp.float32) / length
        return jnp.exp(RATE * centred * centred) * length**-0.5

    @pl.loop(0, devices)
    def _(e):
        at = pl.ds(pl.multiple_of(8 + e * depth, depth), depth)
        field[:, at, :] = real_ref[e] * scale(e * depth, real_ref.shape[1:])

    field[:, 7:8, :] = halo_ref[0][:, None, :] * scale(-1, (GAP, 1, LANES))
    field[:, STEPS + 8 : STEPS + 9, :] = halo_ref[1][:, None, :] * scale(STEPS, (GAP, 1, LANES))

    lane = lax.broadcasted_iota(jnp.int32, (8, LANES), 1)

    @pl.loop(0, STEPS // 8)
    def _(tile):
        row = pl.multiple_of(tile * 8, 8)
        index = index_ref[pl.ds(row, 8)]
        offset = offset_ref[pl.ds(row, 8)]
        samples = {}
        for p in range(GAP):
            now = field[p, pl.ds(row + 8, 8)]
            before = field[p, pl.ds(row + 7, 8)]
            after = field[p, pl.ds(row + 9, 8)]
            for slot in (-2, -1, 0, 1, 2):
                place = GAP * slot + p
                if place < 1 - HALF or place > HALF + GAP - 1:
                    continue
                if slot < 0:
                    value = pltpu.roll(jnp.where(lane >= LANES + slot, before, now), -slot, 1)
                elif slot > 0:
                    value = pltpu.roll(jnp.where(lane < slot, after, now), LANES - slot, 1)
                else:
                    value = now
                samples[place] = value
        window = [samples[place] for place in range(1 - HALF, HALF + GAP)]
        for bit in (4, 2, 1):
            chosen = (index & bit) != 0
            window = [jnp.where(chosen, b, a) for a, b in zip(window[:-bit], window[bit:])]
        total = jnp.zeros((8, LANES), jnp.float32)
        for tap in range(2 * HALF):
            total += window[tap] * jnp.take_along_axis(weight_ref[tap], offset, axis=1)
        gram_ref[pl.ds(row, 8)] = total

    pieces = []
    rest = jnp.concatenate([field[p, 8 : STEPS + 8, :] for p in range(GAP)], axis=1)
    for _ in range(3):
        piece = rest.astype(jnp.bfloat16)
        pieces.append(piece)
        rest = rest - piece.astype(jnp.float32)
    width = 2 * LANES
    for column in range(GAP * LANES // width):
        table = order_ref[:, column * width : (column + 1) * width]
        block = sum(jnp.dot(piece, table, preferred_element_type=jnp.float32) for piece in reversed(pieces))
        for side in range(2):
            z_ref[pl.ds(2 * column + side, STEPS, stride=GAP), :] = block[:, side * LANES : (side + 1) * LANES]


def local(inner, outer, samples, gram_index, gram_offset):
    real, halo = across(samples, inner, outer)
    rows = (STEPS, LANES)
    z, gram = pl.pallas_call(
        functools.partial(gram_kernel, inner, outer),
        out_shape=(
            jax.ShapeDtypeStruct((STEPS * GAP, LANES), jnp.float32),
            jax.ShapeDtypeStruct(rows, jnp.float32),
        ),
        in_specs=[pl.BlockSpec(memory_space=pltpu.VMEM)] * 6,
        out_specs=(pl.BlockSpec(memory_space=pltpu.VMEM),) * 2,
        scratch_shapes=[pltpu.VMEM((GAP, STEPS + 16, LANES), jnp.float32)],
        compiler_params=pltpu.CompilerParams(vmem_limit_bytes=48 * 2**20),
    )(
        real, halo, gram_index.reshape(rows), gram_offset.reshape(rows),
        jnp.asarray(weight_table()), jnp.asarray(order_table()),
    )
    return z.reshape(-1), gram.reshape(-1)


def solution(mesh):
    return jax.shard_map(
        functools.partial(local, mesh.shape["inner"], mesh.shape["outer"]),
        mesh=mesh,
        in_specs=(P(None, ("inner", "outer"), None), P(("inner", "outer")), P(("inner", "outer"))),
        out_specs=(P(("inner", "outer")), P(("inner", "outer"))),
        check_vma=False,
    )
```

profile of v0, /device:TPU:21, one launch (start us, length us, event | category | flops | bytes accessed | tf_op | source)
XLA Modules:
  0.0 101.7 jit_solution(3749446033277736554)
XLA Ops:
  0.7 0.3 fusion.10
  1.0 0.5 fusion.1
  1.5 0.0 copy-start.1
  1.5 1.6 %copy-done.1 = f32[2,1,262144]{2,1,0:T(1,128)S(1)} copy-done((f32[2,1,262144]{2,1,0:T(1,128)S(1)}, f32[2,1,262144]{2,1,0:T(1,128)}, u32[]{:S(2)}) %copy-start.1) | copy-done | bytes 2097176
  3.1 0.0 copy-start
  3.1 0.0 copy-start.2
  3.1 0.0 copy-start.3
  3.1 0.0 copy-start.4
  3.1 90.3 %shard_map.77 = (f32[32,8,8,128]{3,2,1,0:T(8,128)S(1)}, f32[2,8,128]{2,1,0:T(8,128)S(1)}) custom-call(f32[2,8,256,128]{3,2,1,0:T(8,128)S(1)} %bitcast.5, bf16[8,4,256,256]{3,2,1,0:T(8,128)(2,1)} %constant.41.clone.stage_ref, f32[2,256,128]{2,1,0:T(8,128)S(1)} %pad_maximum_fusion.u_ref, f32[2,8,128]{2,1,0:T(8,128)S(1)} %pad_maximum_fusion.1.v_ref, ...), custom_call_target="tpu_custom_call" | custom-call | tf_op jit(solution)/shard_map/pallas_call | solution.py:302
  93.5 0.0 copy-done
  93.5 0.0 copy-done.2
  93.5 0.0 copy-done.3
  93.5 0.0 copy-done.4
  93.5 8.2 %shard_map.78 = (f32[2048,128]{1,0:T(8,128)}, f32[256,128]{1,0:T(8,128)}) custom-call(f32[32,8,8,128]{3,2,1,0:T(8,128)S(1)} %get-tuple-element.6.real_ref, f32[2,8,128]{2,1,0:T(8,128)S(1)} %get-tuple-element.7.halo_ref, s32[256,128]{1,0:T(8,128)S(1)} %bitcast.6, s32[256,128]{1,0:T(8,128)S(1)} %bitcast.7, f32[32,8,128]{2,1,0:T(8,128)S(1)} %copy-done.4, ...), custom_call_target="tpu_custom_call" | custom-call | tf_op jit(solution)/shard_map/pallas_call | solution.py:397
  (5 shorter events, 0.1 us)
Async XLA Ops:
  1.5 1.6 %copy-start.1 = (f32[2,1,262144]{2,1,0:T(1,128)S(1)}, f32[2,1,262144]{2,1,0:T(1,128)}, u32[]{:S(2)}) copy-start(f32[2,1,262144]{2,1,0:T(1,128)} %param.6) | copy-start | bytes 6291460
  3.1 90.4 %copy-start = (bf16[1024,1024]{1,0:T(8,128)(2,1)S(1)}, bf16[1024,1024]{1,0:T(8,128)(2,1)}, u32[]{:S(2)}) copy-start(bf16[1024,1024]{1,0:T(8,128)(2,1)} %constant.43.clone.order_ref) | copy-start | bytes 6291460
  3.1 90.4 %copy-start.2 = (s32[32768]{0:T(1024)S(1)}, s32[32768]{0:T(1024)}, u32[]{:S(2)}) copy-start(s32[32768]{0:T(1024)} %param.7) | copy-start | bytes 393220
  3.1 90.4 %copy-start.3 = (s32[32768]{0:T(1024)S(1)}, s32[32768]{0:T(1024)}, u32[]{:S(2)}) copy-start(s32[32768]{0:T(1024)} %param.8) | copy-start | bytes 393220
  3.1 90.4 %copy-start.4 = (f32[32,8,128]{2,1,0:T(8,128)S(1)}, f32[32,8,128]{2,1,0:T(8,128)}, u32[]{:S(2)}) copy-start(f32[32,8,128]{2,1,0:T(8,128)} %constant.42.clone.weight_ref) | copy-start | bytes 393220
where the time goes:
time: 102 us
  Pallas kernels  98.6 us (97%)
  local copies, waits for them, and re-layouts  1.6 us (2%)
    pallas_call x1, Pallas kernels, across(): pl.pallas_call(functools.partial(across_kernel, inner, outer), out_shape=...  90.3 us
    pallas_call x1, Pallas kernels, local(): pl.pallas_call(functools.partial(gram_kernel, inner, outer), out_shape=(j...  8.22 us

commit v1 on v0

--- a/solution.py
+++ b/solution.py
@@ -15,6 +15,7 @@
 LANES = 128
 RADIX = 8
 STEPS = 256
+GROUPS = 4
 TAU = 2.0 * math.pi
 RATE = 4.0
 MESH = pl.DeviceIdType.MESH
@@ -123,19 +124,24 @@
 ):
     devices = inner * outer
     me = lax.axis_index("inner") * outer + lax.axis_index("outer")
-    depth = send_a.shape[3]
+    groups, half, _, per, depth, _ = send_a.shape
+    side_of = me // half
+    place = me % half
 
     def where(device):
         return (device // outer, device % outer)
 
-    def other(step):
-        return (me + step) % devices
+    def near(step):
+        return side_of * half + (place + step) % half
+
+    def far(step):
+        return (1 - side_of) * half + (place + step) % half
 
     barrier = pltpu.get_barrier_semaphore()
 
     @pl.loop(1, devices)
     def _(step):
-        pl.semaphore_signal(barrier, inc=1, device_id=where(other(step)), device_id_type=MESH)
+        pl.semaphore_signal(barrier, inc=1, device_id=where((me + step) % devices), device_id_type=MESH)
 
     @pl.loop(0, STEPS // 32)
     def _(tile):
@@ -151,10 +157,32 @@
     def dot_nt(a, b):
         return lax.dot_general(a, b, NT, preferred_element_type=jnp.float32)
 
+    def copy_a(group, target, source):
+        return pltpu.make_async_remote_copy(
+            src_ref=send_a.at[group, target % half], dst_ref=recv_a.at[group, place],
+            send_sem=sem_sa.at[group, target % half], recv_sem=sem_ra.at[group, source % half],
+            device_id=where(target), device_id_type=MESH,
+        )
+
+    def copy_b(group, target, source):
+        return pltpu.make_async_remote_copy(
+            src_ref=send_b.at[group, target], dst_ref=out_ref.at[group, me],
+            send_sem=sem_sb.at[group, target], recv_sem=sem_rb.at[group, source],
+            device_id=where(target), device_id_type=MESH,
+        )
+
+    def copy_edge(target, end, source_side):
+        shift = 1 if end else -1
+        return pltpu.make_async_remote_copy(
+            src_ref=edge.at[target + shift], dst_ref=halo_ref.at[end, side_of],
+            send_sem=sem_se.at[target], recv_sem=sem_re.at[end, source_side],
+            device_id=where(target), device_id_type=MESH,
+        )
+
     last_high, last_low = halves(last_ref[...])
 
-    @pl.loop(0, RADIX)
-    def _(p):
+    def spectrum(group, member):
+        p = group * per + member
         high, low = halves(parts[p])
         cos_high, cos_low, sin_high, sin_low = (stage_ref[p, i] for i in range(4))
         by_cos = dot(cos_high, high) + dot(cos_high, low) + dot(cos_low, high)
@@ -169,109 +197,139 @@
         z = dot_nt(last_high, high) + dot_nt(last_high, low) + dot_nt(last_low, high)
         for part in range(2):
             block = z[part * LANES : (part + 1) * LANES]
-            for side in range(2):
-                rows[part, pl.ds(side, LANES, stride=2), :] = block[:, side * LANES : (side + 1) * LANES]
-            send_a[:, part, p] = rows[part].reshape(devices, depth, LANES)
-
-    pl.semaphore_wait(barrier, devices - 1)
-
-    def copy_a(target, source):
-        return pltpu.make_async_remote_copy(
-            src_ref=send_a.at[target], dst_ref=recv_a.at[me],
-            send_sem=sem_sa.at[target], recv_sem=sem_ra.at[source],
-            device_id=where(target), device_id_type=MESH,
-        )
-
-    def copy_b(target, source):
-        return pltpu.make_async_remote_copy(
-            src_ref=send_b.at[target], dst_ref=out_ref.at[me],
-            send_sem=sem_sb.at[target], recv_sem=sem_rb.at[source],
-            device_id=where(target), device_id_type=MESH,
-        )
-
-    def copy_edge(target, side):
-        shift = 1 if side else -1
-        return pltpu.make_async_remote_copy(
-            src_ref=edge.at[target + shift], dst_ref=halo_ref.at[side],
-            send_sem=sem_se.at[target], recv_sem=sem_re.at[side],
-            device_id=where(target), device_id_type=MESH,
-        )
-
-    @pl.loop(1, devices)
-    def _(step):
-        copy_a(other(step), me).start()
-
-    recv_a[me] = send_a[me]
-
-    @pl.loop(1, devices)
-    def _(step):
-        source = other(devices - step)
-        copy_a(source, source).wait_recv()
-
-    @pl.loop(0, RADIX)
-    def _(p):
-        values = [(recv_a[a, 0, p], recv_a[a, 1, p]) for a in range(devices)]
-        done = real_transform(values)
-        for k in range(devices):
-            send_b[k, p] = done[k]
-
-    def fill_edge(row):
+            for lane_half in range(2):
+                rows[part, pl.ds(lane_half, LANES, stride=2), :] = block[:, lane_half * LANES : (lane_half + 1) * LANES]
+            send_a[group, :, part, member] = rows[part].reshape(half, depth, LANES)
+
+    @pl.loop(0, groups)
+    def _(group):
+        @pl.loop(0, per)
+        def _(member):
+            spectrum(group, member)
+
+        @pl.when(group == 0)
+        def _():
+            pl.semaphore_wait(barrier, devices - 1)
+
+        @pl.loop(1, half)
+        def _(step):
+            copy_a(group, near(step), me).start()
+
+        recv_a[group, place] = send_a[group, place]
+
+    sign = (1 - 2 * side_of).astype(jnp.float32)
+
+    def combine(group, member):
+        values = [(recv_a[group, a, 0, member], recv_a[group, a, 1, member]) for a in range(half)]
+        for k, done in enumerate(real_transform(values)):
+            send_b[group, 2 * k, member] = done
+        turned = []
+        for a, (vr, vi) in enumerate(values):
+            c, s = math.cos(TAU * a / devices), -math.sin(TAU * a / devices)
+            cs, ss = sign * c, sign * s
+            turned.append((vr * cs, vi * cs) if a == 0 else (vr * cs - vi * ss, vr * ss + vi * cs))
+        for k, done in enumerate(real_transform(turned)):
+            send_b[group, 2 * k + 1, member] = done
+
+    def edges(end):
+        row = 0 if end else depth - 1
+        shift = 1 if end else -1
+
         @pl.loop(0, devices)
         def _(k):
-            edge[k] = send_b[k, :, row]
-
-    @pl.when(me == 0)
-    def _():
-        fill_edge(0)
-
-        @pl.loop(1, devices - 1)
+            for group in range(groups):
+                edge[k, group * per : (group + 1) * per] = send_b[group, k, :, row]
+
+        @pl.loop(0, devices)
         def _(target):
-            copy_edge(target, 1).start()
-
-    @pl.when(me == devices - 1)
-    def _():
-        fill_edge(depth - 1)
-
-        @pl.loop(1, devices - 1)
+            inside = jnp.logical_and(target + shift >= 0, target + shift < devices)
+
+            @pl.when(jnp.logical_and(inside, target != me))
+            def _():
+                copy_edge(target, end, side_of).start()
+
+    def edges_sent(end):
+        shift = 1 if end else -1
+
+        @pl.loop(0, devices)
         def _(target):
-            copy_edge(target, 0).start()
-
-    @pl.loop(1, devices)
-    def _(step):
-        copy_b(other(step), me).start()
-
-    out_ref[me] = send_b[me]
-
-    @pl.when(me == 0)
-    def _():
-        halo_ref[0] = jnp.zeros(halo_ref.shape[1:], jnp.float32)
-        halo_ref[1] = edge[1]
-
-    @pl.when(me == devices - 1)
-    def _():
-        halo_ref[0] = edge[devices - 2]
-        halo_ref[1] = jnp.zeros(halo_ref.shape[1:], jnp.float32)
-
-    @pl.loop(1, devices)
-    def _(step):
-        source = other(devices - step)
-        copy_b(source, source).wait_recv()
-
-    @pl.when(jnp.logical_and(me > 0, me < devices - 1))
-    def _():
-        copy_edge(me, 0).wait_recv()
-        copy_edge(me, 1).wait_recv()
-
-    @pl.when(jnp.logical_or(me == 0, me == devices - 1))
-    def _():
-        @pl.loop(1, devices - 1)
-        def _(target):
-            copy_edge(target, 0).wait_send()
-
-    @pl.loop(1, devices)
-    def _(step):
-        copy_a(other(step), me).wait_send()
-        copy_b(other(step), me).wait_send()
+            inside = jnp.logical_and(target + shift >= 0, target + shift < devices)
+
+            @pl.when(jnp.logical_and(inside, target != me))
+            def _():
+                copy_edge(target, end, side_of).wait_send()
+
+    @pl.loop(0, groups)
+    def _(group):
+        @pl.loop(1, half)
+        def _(step):
+            source = near(half - step)
+            copy_a(group, source, source).wait_recv()
+
+        @pl.loop(0, per)
+        def _(member):
+            combine(group, member)
+
+        @pl.when(group == groups - 1)
+        def _():
+            for end in range(2):
+                @pl.when(place == (0 if end else half - 1))
+                def _():
+                    edges(end)
+
+        @pl.loop(0, half)
+        def _(step):
+            copy_b(group, far(step), me).start()
+
+        @pl.loop(1, half)
+        def _(step):
+            copy_b(group, near(step), me).start()
+
+        out_ref[group, me] = send_b[group, me]
+
+    for end in range(2):
+        sender = 0 if end else half - 1
+        bound = devices - 1 if end else 0
+        shift = 1 if end else -1
+
+        @pl.when(me == bound)
+        def _():
+            halo_ref[end] = jnp.zeros(halo_ref.shape[1:], jnp.float32)
+
+        @pl.when(me != bound)
+        def _():
+            for source_side in range(2):
+                source = source_side * half + sender
+
+                @pl.when(me == source)
+                def _():
+                    halo_ref[end, source_side] = edge[me + shift]
+
+                @pl.when(me != source)
+                def _():
+                    copy_edge(me, end, source_side).wait_recv()
+
+    @pl.loop(0, groups)
+    def _(group):
+        @pl.loop(1, devices)
+        def _(step):
+            source = (me + devices - step) % devices
+            copy_b(group, source, source).wait_recv()
+
+    for end in range(2):
+        @pl.when(place == (0 if end else half - 1))
+        def _():
+            edges_sent(end)
+
+    @pl.loop(0, groups)
+    def _(group):
+        @pl.loop(1, half)
+        def _(step):
+            copy_a(group, near(step), me).wait_send()
+
+        @pl.loop(1, devices)
+        def _(step):
+            copy_b(group, (me + step) % devices, me).wait_send()
 
 
 def across(samples, inner, outer):
@@ -279,7 +337,9 @@
     seg = samples.shape[2]
     length = seg * devices
     me = lax.axis_index("inner") * outer + lax.axis_index("outer")
-    depth = seg // (devices * RADIX * LANES)
+    half = devices // 2
+    depth = STEPS // half
+    per = RADIX // GROUPS
     x = samples.reshape(2, RADIX, STEPS, LANES)
 
     def phase(number, order):
@@ -298,25 +358,27 @@
         [jnp.concatenate([cosine, -sine], axis=1), jnp.concatenate([sine, cosine], axis=1)], axis=0
     )
     vmem = pl.BlockSpec(memory_space=pltpu.VMEM)
-    block = (devices, RADIX, depth, LANES)
+    first = (GROUPS, half, 2, per, depth, LANES)
+    block = (GROUPS, devices, per, depth, LANES)
     return pl.pallas_call(
         functools.partial(across_kernel, inner, outer),
         out_shape=(
             jax.ShapeDtypeStruct(block, jnp.float32),
-            jax.ShapeDtypeStruct((2, RADIX, LANES), jnp.float32),
+            jax.ShapeDtypeStruct((2, 2, RADIX, LANES), jnp.float32),
         ),
         in_specs=[vmem] * 5,
         out_specs=(vmem, vmem),
         scratch_shapes=[
             pltpu.VMEM((RADIX, STEPS, 2 * LANES), jnp.float32),
             pltpu.VMEM((2, STEPS, LANES), jnp.float32),
-            pltpu.VMEM((devices, 2, RADIX, depth, LANES), jnp.float32),
-            pltpu.VMEM((devices, 2, RADIX, depth, LANES), jnp.float32),
+            pltpu.VMEM(first, jnp.float32),
+            pltpu.VMEM(first, jnp.float32),
             pltpu.VMEM(block, jnp.float32),
             pltpu.VMEM((devices, RADIX, LANES), jnp.float32),
         ]
-        + [pltpu.SemaphoreType.DMA((devices,))] * 5
-        + [pltpu.SemaphoreType.DMA((2,))],
+        + [pltpu.SemaphoreType.DMA((GROUPS, half))] * 2
+        + [pltpu.SemaphoreType.DMA((GROUPS, devices))] * 2
+        + [pltpu.SemaphoreType.DMA((devices,)), pltpu.SemaphoreType.DMA((2, 2))],
         compiler_params=pltpu.CompilerParams(
             collective_id=0, has_side_effects=True, vmem_limit_bytes=48 * 2**20
         ),
@@ -325,7 +387,8 @@
 
 def gram_kernel(inner, outer, real_ref, halo_ref, index_ref, offset_ref, weight_ref, order_ref, z_ref, gram_ref, field):
     devices = inner * outer
-    depth = real_ref.shape[2]
+    groups, _, per, depth, _ = real_ref.shape
+    half = devices // 2
     seg = STEPS * LANES * GAP
     length = seg * devices
     me = lax.axis_index("inner") * outer + lax.axis_index("outer")
@@ -337,13 +400,17 @@
         centred = base + at.astype(jnp.float32) / length
         return jnp.exp(RATE * centred * centred) * length**-0.5
 
-    @pl.loop(0, devices)
+    @pl.loop(0, half)
     def _(e):
-        at = pl.ds(pl.multiple_of(8 + e * depth, depth), depth)
-        field[:, at, :] = real_ref[e] * scale(e * depth, real_ref.shape[1:])
-
-    field[:, 7:8, :] = halo_ref[0][:, None, :] * scale(-1, (GAP, 1, LANES))
-    field[:, STEPS + 8 : STEPS + 9, :] = halo_ref[1][:, None, :] * scale(STEPS, (GAP, 1, LANES))
+        at = pl.ds(pl.multiple_of(8 + e * depth, math.gcd(8, depth)), depth)
+        factor = scale(e * depth, (GAP, depth, LANES))
+        for group in range(groups):
+            members = slice(group * per, (group + 1) * per)
+            field[members, at, :] = (real_ref[group, e] + real_ref[group, half + e]) * factor[members]
+
+    halo = halo_ref[:, 0] + halo_ref[:, 1]
+    field[:, 7:8, :] = halo[0][:, None, :] * scale(-1, (GAP, 1, LANES))
+    field[:, STEPS + 8 : STEPS + 9, :] = halo[1][:, None, :] * scale(STEPS, (GAP, 1, LANES))
 
     lane = lax.broadcasted_iota(jnp.int32, (8, LANES), 1)
 

time: 102 us -> 88.8 us (0.87)
  the two profiles are of different devices: /device:TPU:21 before, /device:TPU:0 now
where the time goes in v1:
time: 88.8 us; the launch traced here: 88.7 us
  Pallas kernels  85.5 us (96%)
  local copies, waits for them, and re-layouts  1.6 us (2%)
    pallas_call x1, Pallas kernels, across(): pl.pallas_call(functools.partial(across_kernel, inner, outer), out_shape=...  77.5 us
    pallas_call x1, Pallas kernels, local(): pl.pallas_call(functools.partial(gram_kernel, inner, outer), out_shape=(j...  8.05 us

profile of v1, /device:TPU:0, one launch (start us, length us, event | category | flops | bytes accessed | tf_op | source)
XLA Modules:
  0.0 88.7 jit_solution(7793760424732636906)
XLA Ops:
  0.7 0.3 fusion.10
  1.0 0.5 fusion.1
  1.5 0.0 copy-start.1
  1.5 1.6 %copy-done.1 = f32[2,1,262144]{2,1,0:T(1,128)S(1)} copy-done((f32[2,1,262144]{2,1,0:T(1,128)S(1)}, f32[2,1,262144]{2,1,0:T(1,128)}, u32[]{:S(2)}) %copy-start.1) | copy-done | bytes 2097176
  3.1 0.0 copy-start
  3.1 0.0 copy-start.2
  3.1 0.0 copy-start.3
  3.1 0.0 copy-start.4
  3.1 77.5 %shard_map.77 = (f32[4,32,2,16,128]{4,3,2,1,0:T(8,128)S(1)}, f32[2,2,8,128]{3,2,1,0:T(8,128)S(1)}) custom-call(f32[2,8,256,128]{3,2,1,0:T(8,128)S(1)} %bitcast.5, bf16[8,4,256,256]{3,2,1,0:T(8,128)(2,1)} %constant.41.clone.stage_ref, f32[2,256,128]{2,1,0:T(8,128)S(1)} %pad_maximum_fusion.u_ref, f32[2,8,128]{2,1,0:T(8,128)S(1)} %pad_maximum_fusion.1.v_ref, ...), custom_call_target="tpu_custom_call" | custom-call | tf_op jit(solution)/shard_map/pallas_call | solution.py:363
  80.6 0.0 copy-done
  80.6 0.0 copy-done.2
  80.6 0.0 copy-done.3
  80.6 0.0 copy-done.4
  80.6 8.0 %shard_map.78 = (f32[2048,128]{1,0:T(8,128)}, f32[256,128]{1,0:T(8,128)}) custom-call(f32[4,32,2,16,128]{4,3,2,1,0:T(8,128)S(1)} %get-tuple-element.6.real_ref, f32[2,2,8,128]{3,2,1,0:T(8,128)S(1)} %get-tuple-element.7.halo_ref, s32[256,128]{1,0:T(8,128)S(1)} %bitcast.6, s32[256,128]{1,0:T(8,128)S(1)} %bitcast.7, f32[32,8,128]{2,1,0:T(8,128)S(1)} %copy-done.4, ...), custom_call_target="tpu_custom_call" | custom-call | tf_op jit(solution)/shard_map/pallas_call | solution.py:464
  (5 shorter events, 0.1 us)
Async XLA Ops:
  1.5 1.6 %copy-start.1 = (f32[2,1,262144]{2,1,0:T(1,128)S(1)}, f32[2,1,262144]{2,1,0:T(1,128)}, u32[]{:S(2)}) copy-start(f32[2,1,262144]{2,1,0:T(1,128)} %param.6) | copy-start | bytes 6291460
  3.1 77.5 %copy-start = (bf16[1024,1024]{1,0:T(8,128)(2,1)S(1)}, bf16[1024,1024]{1,0:T(8,128)(2,1)}, u32[]{:S(2)}) copy-start(bf16[1024,1024]{1,0:T(8,128)(2,1)} %constant.43.clone.order_ref) | copy-start | bytes 6291460
  3.1 77.5 %copy-start.2 = (s32[32768]{0:T(1024)S(1)}, s32[32768]{0:T(1024)}, u32[]{:S(2)}) copy-start(s32[32768]{0:T(1024)} %param.7) | copy-start | bytes 393220
  3.1 77.5 %copy-start.3 = (s32[32768]{0:T(1024)S(1)}, s32[32768]{0:T(1024)}, u32[]{:S(2)}) copy-start(s32[32768]{0:T(1024)} %param.8) | copy-start | bytes 393220
  3.1 77.5 %copy-start.4 = (f32[32,8,128]{2,1,0:T(8,128)S(1)}, f32[32,8,128]{2,1,0:T(8,128)}, u32[]{:S(2)}) copy-start(f32[32,8,128]{2,1,0:T(8,128)} %constant.42.clone.weight_ref) | copy-start | bytes 393220

commit v2 on v1

--- a/solution.py
+++ b/solution.py
@@ -15,7 +15,8 @@
 LANES = 128
 RADIX = 8
 STEPS = 256
-GROUPS = 4
+GROUPS = 8
+AHEAD = 2
 TAU = 2.0 * math.pi
 RATE = 4.0
 MESH = pl.DeviceIdType.MESH
@@ -157,18 +158,26 @@
     def dot_nt(a, b):
         return lax.dot_general(a, b, NT, preferred_element_type=jnp.float32)
 
-    def copy_a(group, target, source):
+    def copy_a(group, target):
         return pltpu.make_async_remote_copy(
             src_ref=send_a.at[group, target % half], dst_ref=recv_a.at[group, place],
-            send_sem=sem_sa.at[group, target % half], recv_sem=sem_ra.at[group, source % half],
+            send_sem=sem_sa.at[group], recv_sem=sem_ra.at[group],
             device_id=where(target), device_id_type=MESH,
         )
 
-    def copy_b(group, target, source):
+    def copy_b(group, target):
         return pltpu.make_async_remote_copy(
             src_ref=send_b.at[group, target], dst_ref=out_ref.at[group, me],
-            send_sem=sem_sb.at[group, target], recv_sem=sem_rb.at[group, source],
+            send_sem=sem_sb.at[group], recv_sem=sem_rb.at[group],
             device_id=where(target), device_id_type=MESH,
+        )
+
+    def whole(ref, group, sem_sent, sem_here):
+        count = ref.shape[1] - 1
+        return pltpu.make_async_remote_copy(
+            src_ref=ref.at[group, pl.ds(0, count)], dst_ref=ref.at[group, pl.ds(0, count)],
+            send_sem=sem_sent.at[group], recv_sem=sem_here.at[group],
+            device_id=where((me + 1) % devices), device_id_type=MESH,
         )
 
     def copy_edge(target, end, source_side):
@@ -201,21 +210,25 @@
                 rows[part, pl.ds(lane_half, LANES, stride=2), :] = block[:, lane_half * LANES : (lane_half + 1) * LANES]
             send_a[group, :, part, member] = rows[part].reshape(half, depth, LANES)
 
-    @pl.loop(0, groups)
-    def _(group):
+    def spectra(group):
         @pl.loop(0, per)
         def _(member):
             spectrum(group, member)
 
-        @pl.when(group == 0)
-        def _():
-            pl.semaphore_wait(barrier, devices - 1)
+        recv_a[group, place] = send_a[group, place]
+
+    spectra(0)
+    pl.semaphore_wait(barrier, devices - 1)
+
+    @pl.loop(0, AHEAD)
+    def _(group):
+        @pl.when(group > 0)
+        def _():
+            spectra(group)
 
         @pl.loop(1, half)
         def _(step):
-            copy_a(group, near(step), me).start()
-
-        recv_a[group, place] = send_a[group, place]
+            copy_a(group, near(step)).start()
 
     sign = (1 - 2 * side_of).astype(jnp.float32)
 
@@ -261,10 +274,11 @@
 
     @pl.loop(0, groups)
     def _(group):
-        @pl.loop(1, half)
-        def _(step):
-            source = near(half - step)
-            copy_a(group, source, source).wait_recv()
+        @pl.when(group + AHEAD < groups)
+        def _():
+            spectra(group + AHEAD)
+
+        whole(recv_a, group, sem_sa, sem_ra).wait_recv()
 
         @pl.loop(0, per)
         def _(member):
@@ -277,13 +291,16 @@
                 def _():
                     edges(end)
 
-        @pl.loop(0, half)
-        def _(step):
-            copy_b(group, far(step), me).start()
+        copy_b(group, far(0)).start()
 
         @pl.loop(1, half)
         def _(step):
-            copy_b(group, near(step), me).start()
+            copy_b(group, far(step)).start()
+            copy_b(group, near(step)).start()
+
+            @pl.when(group + AHEAD < groups)
+            def _():
+                copy_a(group + AHEAD, near(step)).start()
 
         out_ref[group, me] = send_b[group, me]
 
@@ -311,10 +328,7 @@
 
     @pl.loop(0, groups)
     def _(group):
-        @pl.loop(1, devices)
-        def _(step):
-            source = (me + devices - step) % devices
-            copy_b(group, source, source).wait_recv()
+        whole(out_ref, group, sem_sb, sem_rb).wait_recv()
 
     for end in range(2):
         @pl.when(place == (0 if end else half - 1))
@@ -323,13 +337,8 @@
 
     @pl.loop(0, groups)
     def _(group):
-        @pl.loop(1, half)
-        def _(step):
-            copy_a(group, near(step), me).wait_send()
-
-        @pl.loop(1, devices)
-        def _(step):
-            copy_b(group, (me + step) % devices, me).wait_send()
+        whole(send_a, group, sem_sa, sem_ra).wait_send()
+        whole(send_b, group, sem_sb, sem_rb).wait_send()
 
 
 def across(samples, inner, outer):
@@ -376,8 +385,7 @@
             pltpu.VMEM(block, jnp.float32),
             pltpu.VMEM((devices, RADIX, LANES), jnp.float32),
         ]
-        + [pltpu.SemaphoreType.DMA((GROUPS, half))] * 2
-        + [pltpu.SemaphoreType.DMA((GROUPS, devices))] * 2
+        + [pltpu.SemaphoreType.DMA((GROUPS,))] * 4
         + [pltpu.SemaphoreType.DMA((devices,)), pltpu.SemaphoreType.DMA((2, 2))],
         compiler_params=pltpu.CompilerParams(
             collective_id=0, has_side_effects=True, vmem_limit_bytes=48 * 2**20

time: 88.8 us -> 81.2 us (0.914)
  Pallas kernels: 85.5 us -> 77.9 us
    pallas_call x1, Pallas kernels: 77.5 us -> 69.9 us  [across(): pl.pallas_call(functools.partial(across_kernel, inner, outer), out_shape=...]
where the time goes in v2:
time: 81.2 us; the launch traced here: 81.1 us
  Pallas kernels  77.9 us (96%)
  local copies, waits for them, and re-layouts  1.6 us (2%)
  other arithmetic  0.85 us (1%)
    pallas_call x1, Pallas kernels, across(): pl.pallas_call(functools.partial(across_kernel, inner, outer), out_shape=...  69.9 us
    pallas_call x1, Pallas kernels, local(): pl.pallas_call(functools.partial(gram_kernel, inner, outer), out_shape=(j...  8.04 us

profile of v2, /device:TPU:0, one launch (start us, length us, event | category | flops | bytes accessed | tf_op | source)
XLA Modules:
  0.0 81.1 jit_solution(11237422286660165182)
XLA Ops:
  0.7 0.3 fusion.10
  1.0 0.5 fusion.1
  1.5 0.0 copy-start.1
  1.5 1.6 %copy-done.1 = f32[2,1,262144]{2,1,0:T(1,128)S(1)} copy-done((f32[2,1,262144]{2,1,0:T(1,128)S(1)}, f32[2,1,262144]{2,1,0:T(1,128)}, u32[]{:S(2)}) %copy-start.1) | copy-done | bytes 2097176
  3.1 0.0 copy-start
  3.1 0.0 copy-start.2
  3.1 0.0 copy-start.3
  3.1 0.0 copy-start.4
  3.1 69.9 %shard_map.77 = (f32[8,32,1,16,128]{4,3,2,1,0:T(8,128)S(1)}, f32[2,2,8,128]{3,2,1,0:T(8,128)S(1)}) custom-call(f32[2,8,256,128]{3,2,1,0:T(8,128)S(1)} %bitcast.5, bf16[8,4,256,256]{3,2,1,0:T(8,128)(2,1)} %constant.41.clone.stage_ref, f32[2,256,128]{2,1,0:T(8,128)S(1)} %pad_maximum_fusion.u_ref, f32[2,8,128]{2,1,0:T(8,128)S(1)} %pad_maximum_fusion.1.v_ref, ...), custom_call_target="tpu_custom_call" | custom-call | tf_op jit(solution)/shard_map/pallas_call | solution.py:372
  73.0 0.0 copy-done
  73.0 0.0 copy-done.2
  73.0 0.0 copy-done.3
  73.0 0.0 copy-done.4
  73.0 8.0 %shard_map.78 = (f32[2048,128]{1,0:T(8,128)}, f32[256,128]{1,0:T(8,128)}) custom-call(f32[8,32,1,16,128]{4,3,2,1,0:T(8,128)S(1)} %get-tuple-element.6.real_ref, f32[2,2,8,128]{3,2,1,0:T(8,128)S(1)} %get-tuple-element.7.halo_ref, s32[256,128]{1,0:T(8,128)S(1)} %bitcast.6, s32[256,128]{1,0:T(8,128)S(1)} %bitcast.7, f32[32,8,128]{2,1,0:T(8,128)S(1)} %copy-done.4, ...), custom_call_target="tpu_custom_call" | custom-call | tf_op jit(solution)/shard_map/pallas_call | solution.py:472
  (5 shorter events, 0.1 us)
Async XLA Ops:
  1.5 1.6 %copy-start.1 = (f32[2,1,262144]{2,1,0:T(1,128)S(1)}, f32[2,1,262144]{2,1,0:T(1,128)}, u32[]{:S(2)}) copy-start(f32[2,1,262144]{2,1,0:T(1,128)} %param.6) | copy-start | bytes 6291460
  3.1 69.9 %copy-start = (bf16[1024,1024]{1,0:T(8,128)(2,1)S(1)}, bf16[1024,1024]{1,0:T(8,128)(2,1)}, u32[]{:S(2)}) copy-start(bf16[1024,1024]{1,0:T(8,128)(2,1)} %constant.43.clone.order_ref) | copy-start | bytes 6291460
  3.1 69.9 %copy-start.2 = (s32[32768]{0:T(1024)S(1)}, s32[32768]{0:T(1024)}, u32[]{:S(2)}) copy-start(s32[32768]{0:T(1024)} %param.7) | copy-start | bytes 393220
  3.1 69.9 %copy-start.3 = (s32[32768]{0:T(1024)S(1)}, s32[32768]{0:T(1024)}, u32[]{:S(2)}) copy-start(s32[32768]{0:T(1024)} %param.8) | copy-start | bytes 393220
  3.1 69.9 %copy-start.4 = (f32[32,8,128]{2,1,0:T(8,128)S(1)}, f32[32,8,128]{2,1,0:T(8,128)}, u32[]{:S(2)}) copy-start(f32[32,8,128]{2,1,0:T(8,128)} %constant.42.clone.weight_ref) | copy-start | bytes 393220

commit v3 on v2

--- a/solution.py
+++ b/solution.py
@@ -46,8 +46,8 @@
 
 
 def order_table():
-    size = GAP * LANES
-    p, l = np.divmod(np.arange(size), LANES)
+    size = 2 * LANES
+    p, l = np.divmod(np.arange(size), size // GAP)
     table = np.zeros((size, size), np.float32)
     table[np.arange(size), GAP * l + p] = 1.0
     return table.astype(jnp.bfloat16)
@@ -120,8 +120,9 @@
 
 
 def across_kernel(
-    inner, outer, x_ref, stage_ref, u_ref, v_ref, last_ref, out_ref, halo_ref,
-    parts, rows, send_a, recv_a, send_b, edge, sem_sa, sem_ra, sem_sb, sem_rb, sem_se, sem_re,
+    inner, outer, x_hbm, stage_hbm, u_ref, v_ref, last_ref, out_ref, halo_ref,
+    x_ref, stage_ref, parts, rows, send_a, recv_a, send_b, edge,
+    sem_x, sem_t, sem_sa, sem_ra, sem_sb, sem_rb, sem_se, sem_re,
 ):
     devices = inner * outer
     me = lax.axis_index("inner") * outer + lax.axis_index("outer")
@@ -138,11 +139,27 @@
     def far(step):
         return (1 - side_of) * half + (place + step) % half
 
+    def load_x(part):
+        return pltpu.make_async_copy(x_hbm.at[part], x_ref.at[part], sem_x.at[part])
+
+    def load_table(p):
+        return pltpu.make_async_copy(stage_hbm.at[p], stage_ref.at[p], sem_t.at[p])
+
+    for part in range(2):
+        load_x(part).start()
+
+    @pl.loop(0, RADIX)
+    def _(p):
+        load_table(p).start()
+
     barrier = pltpu.get_barrier_semaphore()
 
     @pl.loop(1, devices)
     def _(step):
         pl.semaphore_signal(barrier, inc=1, device_id=where((me + step) % devices), device_id_type=MESH)
+
+    for part in range(2):
+        load_x(part).wait()
 
     @pl.loop(0, STEPS // 32)
     def _(tile):
@@ -192,6 +209,7 @@
 
     def spectrum(group, member):
         p = group * per + member
+        load_table(p).wait()
         high, low = halves(parts[p])
         cos_high, cos_low, sin_high, sin_low = (stage_ref[p, i] for i in range(4))
         by_cos = dot(cos_high, high) + dot(cos_high, low) + dot(cos_low, high)
@@ -232,17 +250,28 @@
 
     sign = (1 - 2 * side_of).astype(jnp.float32)
 
+    shape = (depth, LANES)
+    row = lax.broadcasted_iota(jnp.int32, shape, 0) + place * depth
+    slot = (row * LANES + lax.broadcasted_iota(jnp.int32, shape, 1)) * GAP
+    length = STEPS * LANES * GAP * devices
+
     def combine(group, member):
+        within = (slot + (group * per + member)).astype(jnp.float32) / length
+
+        def weighted(k, value):
+            centred = (k / devices - 0.5) + within
+            return value * (jnp.exp(RATE * centred * centred) * length**-0.5)
+
         values = [(recv_a[group, a, 0, member], recv_a[group, a, 1, member]) for a in range(half)]
         for k, done in enumerate(real_transform(values)):
-            send_b[group, 2 * k, member] = done
+            send_b[group, 2 * k, member] = weighted(2 * k, done)
         turned = []
         for a, (vr, vi) in enumerate(values):
             c, s = math.cos(TAU * a / devices), -math.sin(TAU * a / devices)
             cs, ss = sign * c, sign * s
             turned.append((vr * cs, vi * cs) if a == 0 else (vr * cs - vi * ss, vr * ss + vi * cs))
         for k, done in enumerate(real_transform(turned)):
-            send_b[group, 2 * k + 1, member] = done
+            send_b[group, 2 * k + 1, member] = weighted(2 * k + 1, done)
 
     def edges(end):
         row = 0 if end else depth - 1
@@ -375,9 +404,11 @@
             jax.ShapeDtypeStruct(block, jnp.float32),
             jax.ShapeDtypeStruct((2, 2, RADIX, LANES), jnp.float32),
         ),
-        in_specs=[vmem] * 5,
+        in_specs=[pl.BlockSpec(memory_space=pltpu.HBM)] * 2 + [vmem] * 3,
         out_specs=(vmem, vmem),
         scratch_shapes=[
+            pltpu.VMEM(x.shape, jnp.float32),
+            pltpu.VMEM((RADIX, 4, STEPS, STEPS), jnp.bfloat16),
             pltpu.VMEM((RADIX, STEPS, 2 * LANES), jnp.float32),
             pltpu.VMEM((2, STEPS, LANES), jnp.float32),
             pltpu.VMEM(first, jnp.float32),
@@ -385,6 +416,7 @@
             pltpu.VMEM(block, jnp.float32),
             pltpu.VMEM((devices, RADIX, LANES), jnp.float32),
         ]
+        + [pltpu.SemaphoreType.DMA((2,)), pltpu.SemaphoreType.DMA((RADIX,))]
         + [pltpu.SemaphoreType.DMA((GROUPS,))] * 4
         + [pltpu.SemaphoreType.DMA((devices,)), pltpu.SemaphoreType.DMA((2, 2))],
         compiler_params=pltpu.CompilerParams(
@@ -397,32 +429,21 @@
     devices = inner * outer
     groups, _, per, depth, _ = real_ref.shape
     half = devices // 2
-    seg = STEPS * LANES * GAP
-    length = seg * devices
-    me = lax.axis_index("inner") * outer + lax.axis_index("outer")
-    base = me.astype(jnp.float32) / devices - 0.5
-
-    def scale(first_row, shape):
-        row = lax.broadcasted_iota(jnp.int32, shape, 1) + first_row
-        at = (row * LANES + lax.broadcasted_iota(jnp.int32, shape, 2)) * GAP + lax.broadcasted_iota(jnp.int32, shape, 0)
-        centred = base + at.astype(jnp.float32) / length
-        return jnp.exp(RATE * centred * centred) * length**-0.5
 
     @pl.loop(0, half)
     def _(e):
         at = pl.ds(pl.multiple_of(8 + e * depth, math.gcd(8, depth)), depth)
-        factor = scale(e * depth, (GAP, depth, LANES))
         for group in range(groups):
             members = slice(group * per, (group + 1) * per)
-            field[members, at, :] = (real_ref[group, e] + real_ref[group, half + e]) * factor[members]
+            field[members, at, :] = real_ref[group, e] + real_ref[group, half + e]
 
     halo = halo_ref[:, 0] + halo_ref[:, 1]
-    field[:, 7:8, :] = halo[0][:, None, :] * scale(-1, (GAP, 1, LANES))
-    field[:, STEPS + 8 : STEPS + 9, :] = halo[1][:, None, :] * scale(STEPS, (GAP, 1, LANES))
+    field[:, 7:8, :] = halo[0][:, None, :]
+    field[:, STEPS + 8 : STEPS + 9, :] = halo[1][:, None, :]
 
     lane = lax.broadcasted_iota(jnp.int32, (8, LANES), 1)
 
-    @pl.loop(0, STEPS // 8)
+    @pl.loop(0, STEPS // 8, unroll=2)
     def _(tile):
         row = pl.multiple_of(tile * 8, 8)
         index = index_ref[pl.ds(row, 8)]
@@ -452,16 +473,26 @@
             total += window[tap] * jnp.take_along_axis(weight_ref[tap], offset, axis=1)
         gram_ref[pl.ds(row, 8)] = total
 
-    pieces = []
-    rest = jnp.concatenate([field[p, 8 : STEPS + 8, :] for p in range(GAP)], axis=1)
-    for _ in range(3):
-        piece = rest.astype(jnp.bfloat16)
-        pieces.append(piece)
-        rest = rest - piece.astype(jnp.float32)
     width = 2 * LANES
-    for column in range(GAP * LANES // width):
-        table = order_ref[:, column * width : (column + 1) * width]
-        block = sum(jnp.dot(piece, table, preferred_element_type=jnp.float32) for piece in reversed(pieces))
+    share = width // GAP
+    run = lax.broadcasted_iota(jnp.int32, (STEPS, LANES), 1) // share
+    for column in range(LANES // share):
+        packed = []
+        for first in range(0, GAP, LANES // share):
+            piece = None
+            for place in range(LANES // share):
+                value = field[first + place, 8 : STEPS + 8, :]
+                turn = (place - column) * share % LANES
+                value = pltpu.roll(value, turn, 1) if turn else value
+                piece = value if piece is None else jnp.where(run == place, value, piece)
+            packed.append(piece)
+        rest = jnp.concatenate(packed, axis=1)
+        block = None
+        for _ in range(3):
+            piece = rest.astype(jnp.bfloat16)
+            rest = rest - piece.astype(jnp.float32)
+            product = jnp.dot(piece, order_ref[...], preferred_element_type=jnp.float32)
+            block = product if block is None else block + product
         for side in range(2):
             z_ref[pl.ds(2 * column + side, STEPS, stride=GAP), :] = block[:, side * LANES : (side + 1) * LANES]
 

time: 81.2 us -> 77.3 us (0.952)
  Pallas kernels: 77.9 us -> 74 us
    pallas_call x1, Pallas kernels: 8.04 us -> 5.74 us  [local(): pl.pallas_call(functools.partial(gram_kernel, inner, outer), out_shape=(j...]
    pallas_call x1, Pallas kernels: 69.9 us -> 68.3 us  [across(): pl.pallas_call(functools.partial(across_kernel, inner, outer), out_shape=...]
where the time goes in v3:
time: 77.3 us; the launch traced here: 77.2 us
  Pallas kernels  74 us (96%)
  local copies, waits for them, and re-layouts  1.6 us (2%)
  other arithmetic  0.85 us (1%)
    pallas_call x1, Pallas kernels, across(): pl.pallas_call(functools.partial(across_kernel, inner, outer), out_shape=...  68.3 us
    pallas_call x1, Pallas kernels, local(): pl.pallas_call(functools.partial(gram_kernel, inner, outer), out_shape=(j...  5.74 us
    unnamed x10, local copies, waits for them, and re-layouts  1.6 us

profile of v3, /device:TPU:0, one launch (start us, length us, event | category | flops | bytes accessed | tf_op | source)
XLA Modules:
  0.0 77.2 jit_solution(6317673835355151108)
XLA Ops:
  0.7 0.3 fusion.10
  1.0 0.5 fusion.1
  1.5 0.0 copy-start
  1.5 1.6 %copy-done = f32[2,1,262144]{2,1,0:T(1,128)S(1)} copy-done((f32[2,1,262144]{2,1,0:T(1,128)S(1)}, f32[2,1,262144]{2,1,0:T(1,128)}, u32[]{:S(2)}) %copy-start) | copy-done | bytes 2097176
  3.1 0.0 copy-start.1
  3.1 0.0 copy-start.2
  3.1 0.0 copy-start.3
  3.1 0.0 copy-start.4
  3.1 68.3 %shard_map.77 = (f32[8,32,1,16,128]{4,3,2,1,0:T(8,128)S(1)}, f32[2,2,8,128]{3,2,1,0:T(8,128)S(1)}) custom-call(f32[2,8,256,128]{3,2,1,0:T(8,128)S(1)} %bitcast.5, bf16[8,4,256,256]{3,2,1,0:T(8,128)(2,1)} %constant.41.clone.stage_hbm, f32[2,256,128]{2,1,0:T(8,128)S(1)} %pad_maximum_fusion.u_ref, f32[2,8,128]{2,1,0:T(8,128)S(1)} %pad_maximum_fusion.1.v_ref, ...), custom_call_target="tpu_custom_call" | custom-call | tf_op jit(solution)/shard_map/pallas_call | solution.py:401
  71.4 0.0 copy-done.1
  71.4 0.0 copy-done.2
  71.4 0.0 copy-done.3
  71.4 0.0 copy-done.4
  71.4 5.7 %shard_map.78 = (f32[2048,128]{1,0:T(8,128)}, f32[256,128]{1,0:T(8,128)}) custom-call(f32[8,32,1,16,128]{4,3,2,1,0:T(8,128)S(1)} %get-tuple-element.6.real_ref, f32[2,2,8,128]{3,2,1,0:T(8,128)S(1)} %get-tuple-element.7.halo_ref, s32[256,128]{1,0:T(8,128)S(1)} %bitcast.6, s32[256,128]{1,0:T(8,128)S(1)} %bitcast.7, f32[32,8,128]{2,1,0:T(8,128)S(1)} %copy-done.4, ...), custom_call_target="tpu_custom_call" | custom-call | tf_op jit(solution)/shard_map/pallas_call | solution.py:503
  (5 shorter events, 0.1 us)
Async XLA Ops:
  1.5 1.6 %copy-start = (f32[2,1,262144]{2,1,0:T(1,128)S(1)}, f32[2,1,262144]{2,1,0:T(1,128)}, u32[]{:S(2)}) copy-start(f32[2,1,262144]{2,1,0:T(1,128)} %param.6) | copy-start | bytes 6291460
  3.1 68.3 %copy-start.1 = (s32[32768]{0:T(1024)S(1)}, s32[32768]{0:T(1024)}, u32[]{:S(2)}) copy-start(s32[32768]{0:T(1024)} %param.7) | copy-start | bytes 393220
  3.1 68.3 %copy-start.2 = (s32[32768]{0:T(1024)S(1)}, s32[32768]{0:T(1024)}, u32[]{:S(2)}) copy-start(s32[32768]{0:T(1024)} %param.8) | copy-start | bytes 393220
  3.1 68.3 %copy-start.3 = (bf16[256,256]{1,0:T(8,128)(2,1)S(1)}, bf16[256,256]{1,0:T(8,128)(2,1)}, u32[]{:S(2)}) copy-start(bf16[256,256]{1,0:T(8,128)(2,1)} %constant.43.clone.order_ref) | copy-start | bytes 393220
  3.1 68.3 %copy-start.4 = (f32[32,8,128]{2,1,0:T(8,128)S(1)}, f32[32,8,128]{2,1,0:T(8,128)}, u32[]{:S(2)}) copy-start(f32[32,8,128]{2,1,0:T(8,128)} %constant.42.clone.weight_ref) | copy-start | bytes 393220

commit v4 on v3

--- a/solution.py
+++ b/solution.py
@@ -16,7 +16,6 @@
 RADIX = 8
 STEPS = 256
 GROUPS = 8
-AHEAD = 2
 TAU = 2.0 * math.pi
 RATE = 4.0
 MESH = pl.DeviceIdType.MESH
@@ -121,23 +120,25 @@
 
 def across_kernel(
     inner, outer, x_hbm, stage_hbm, u_ref, v_ref, last_ref, out_ref, halo_ref,
-    x_ref, stage_ref, parts, rows, send_a, recv_a, send_b, edge,
-    sem_x, sem_t, sem_sa, sem_ra, sem_sb, sem_rb, sem_se, sem_re,
+    x_ref, stage_ref, parts, rows, send_a, recv_a, raw, own, both, arrived, total, edge,
+    sem_x, sem_t, sem_sa, sem_ra, sem_sw, sem_rw, sem_sp, sem_rp, sem_sb, sem_rb, sem_se, sem_re,
 ):
     devices = inner * outer
     me = lax.axis_index("inner") * outer + lax.axis_index("outer")
-    groups, half, _, per, depth, _ = send_a.shape
-    side_of = me // half
-    place = me % half
+    groups, quarter, _, per, depth, _ = send_a.shape
+    plane = me // quarter
+    place = me % quarter
+    near_plane = plane + 1 - 2 * (plane % 2)
+    far_plane = 3 - plane
+    far_outer = far_plane + 1 - 2 * (far_plane % 2)
+    is_outer = jnp.logical_or(plane == 0, plane == 3)
+    is_inner = jnp.logical_not(is_outer)
 
     def where(device):
         return (device // outer, device % outer)
 
-    def near(step):
-        return side_of * half + (place + step) % half
-
-    def far(step):
-        return (1 - side_of) * half + (place + step) % half
+    def beside(step):
+        return plane * quarter + (place + step) % quarter
 
     def load_x(part):
         return pltpu.make_async_copy(x_hbm.at[part], x_ref.at[part], sem_x.at[part])
@@ -175,35 +176,49 @@
     def dot_nt(a, b):
         return lax.dot_general(a, b, NT, preferred_element_type=jnp.float32)
 
+    def send(source, target_ref, sent, here, device):
+        return pltpu.make_async_remote_copy(
+            src_ref=source, dst_ref=target_ref, send_sem=sent, recv_sem=here,
+            device_id=where(device), device_id_type=MESH,
+        )
+
     def copy_a(group, target):
-        return pltpu.make_async_remote_copy(
-            src_ref=send_a.at[group, target % half], dst_ref=recv_a.at[group, place],
-            send_sem=sem_sa.at[group], recv_sem=sem_ra.at[group],
-            device_id=where(target), device_id_type=MESH,
+        return send(
+            send_a.at[group, target % quarter], recv_a.at[group, place], sem_sa.at[group], sem_ra.at[group], target
         )
 
     def copy_b(group, target):
-        return pltpu.make_async_remote_copy(
-            src_ref=send_b.at[group, target], dst_ref=out_ref.at[group, me],
-            send_sem=sem_sb.at[group], recv_sem=sem_rb.at[group],
-            device_id=where(target), device_id_type=MESH,
+        return send(
+            total.at[group, target % quarter], out_ref.at[group, place], sem_sb.at[group], sem_rb.at[group], target
         )
 
+    def copy_raw(group):
+        return send(
+            recv_a.at[group], raw.at[group], sem_sw.at[group], sem_rw.at[group], near_plane * quarter + place
+        )
+
+    def copy_part(source, group, slot, number, to_plane):
+        return send(
+            source.at[group, pl.ds(to_plane * quarter, quarter)], arrived.at[group, slot],
+            sem_sp.at[group, number], sem_rp.at[group, slot], to_plane * quarter + place,
+        )
+
+    def copy_far(group):
+        return copy_part(both, group, 0, 0, far_plane)
+
+    def copy_far_outer(group):
+        return copy_part(both, group, 0, 1, far_outer)
+
+    def copy_near(group):
+        return copy_part(own, group, 1, 2, near_plane)
+
     def whole(ref, group, sem_sent, sem_here):
-        count = ref.shape[1] - 1
-        return pltpu.make_async_remote_copy(
-            src_ref=ref.at[group, pl.ds(0, count)], dst_ref=ref.at[group, pl.ds(0, count)],
-            send_sem=sem_sent.at[group], recv_sem=sem_here.at[group],
-            device_id=where((me + 1) % devices), device_id_type=MESH,
-        )
-
-    def copy_edge(target, end, source_side):
-        shift = 1 if end else -1
-        return pltpu.make_async_remote_copy(
-            src_ref=edge.at[target + shift], dst_ref=halo_ref.at[end, side_of],
-            send_sem=sem_se.at[target], recv_sem=sem_re.at[end, source_side],
-            device_id=where(target), device_id_type=MESH,
-        )
+        part = ref.at[group, pl.ds(0, quarter - 1)]
+        return send(part, part, sem_sent.at[group], sem_here.at[group], beside(1))
+
+    def copy_edge(kk, end):
+        target = (plane * quarter + kk - (1 if end else -1) + devices) % devices
+        return send(edge.at[kk], halo_ref.at[end], sem_se.at[kk], sem_re.at[end], target)
 
     last_high, last_low = halves(last_ref[...])
 
@@ -226,7 +241,7 @@
             block = z[part * LANES : (part + 1) * LANES]
             for lane_half in range(2):
                 rows[part, pl.ds(lane_half, LANES, stride=2), :] = block[:, lane_half * LANES : (lane_half + 1) * LANES]
-            send_a[group, :, part, member] = rows[part].reshape(half, depth, LANES)
+            send_a[group, :, part, member] = rows[part].reshape(quarter, depth, LANES)
 
     def spectra(group):
         @pl.loop(0, per)
@@ -235,139 +250,206 @@
 
         recv_a[group, place] = send_a[group, place]
 
-    spectra(0)
-    pl.semaphore_wait(barrier, devices - 1)
-
-    @pl.loop(0, AHEAD)
-    def _(group):
-        @pl.when(group > 0)
-        def _():
-            spectra(group)
-
-        @pl.loop(1, half)
+    def factors(which):
+        pairs = []
+        for v in range(4):
+            turns = (which * v) % 4
+            real = jnp.where(turns == 0, 1.0, jnp.where(turns == 2, -1.0, 0.0))
+            imag = jnp.where(turns == 1, -1.0, jnp.where(turns == 3, 1.0, 0.0))
+            pairs.append((real, imag))
+        return pairs
+
+    def outputs(values, pairs):
+        result = [None] * devices
+        for v in range(4):
+            turned = []
+            for a, (vr, vi) in enumerate(values):
+                c, s = math.cos(TAU * a * v / devices), -math.sin(TAU * a * v / devices)
+                turned.append((vr, vi) if a * v == 0 else (vr * c - vi * s, vr * s + vi * c))
+            for u, (real, imag) in enumerate(transform(turned)):
+                result[4 * u + v] = real if v == 0 else real * pairs[v][0] - imag * pairs[v][1]
+        return result
+
+    tall = min(8, depth)
+
+    def tiles(body):
+        @pl.loop(0, per)
+        def _(member):
+            @pl.loop(0, depth // tall)
+            def _(tile):
+                body(member, pl.ds(pl.multiple_of(tile * tall, tall), tall), tile * tall)
+
+    own_pairs, near_pairs = factors(plane), factors(near_plane)
+
+    def first_stage(group):
+        spectra(group)
+
+        @pl.when(group == 0)
+        def _():
+            pl.semaphore_wait(barrier, devices - 1)
+
+        @pl.loop(1, quarter)
         def _(step):
-            copy_a(group, near(step)).start()
-
-    sign = (1 - 2 * side_of).astype(jnp.float32)
-
-    shape = (depth, LANES)
-    row = lax.broadcasted_iota(jnp.int32, shape, 0) + place * depth
-    slot = (row * LANES + lax.broadcasted_iota(jnp.int32, shape, 1)) * GAP
+            copy_a(group, beside(step)).start()
+
+    def second_stage(group):
+        whole(recv_a, group, sem_sa, sem_ra).wait_recv()
+
+        @pl.when(is_outer)
+        def _():
+            copy_raw(group).start()
+
+        def body(member, at, first):
+            values = [(recv_a[group, a, 0, member, at], recv_a[group, a, 1, member, at]) for a in range(quarter)]
+            for k, done in enumerate(outputs(values, own_pairs)):
+                own[group, k, member, at] = done
+
+        tiles(body)
+
+        @pl.when(is_inner)
+        def _():
+            copy_near(group).start()
+
+    def third_stage(group):
+        @pl.when(is_inner)
+        def _():
+            copy_raw(group).wait_recv()
+
+            def body(member, at, first):
+                values = [(raw[group, a, 0, member, at], raw[group, a, 1, member, at]) for a in range(quarter)]
+                for k, done in enumerate(outputs(values, near_pairs)):
+                    both[group, k, member, at] = done + own[group, k, member, at]
+
+            tiles(body)
+            copy_far(group).start()
+            copy_far_outer(group).start()
+
     length = STEPS * LANES * GAP * devices
-
-    def combine(group, member):
-        within = (slot + (group * per + member)).astype(jnp.float32) / length
-
-        def weighted(k, value):
-            centred = (k / devices - 0.5) + within
-            return value * (jnp.exp(RATE * centred * centred) * length**-0.5)
-
-        values = [(recv_a[group, a, 0, member], recv_a[group, a, 1, member]) for a in range(half)]
-        for k, done in enumerate(real_transform(values)):
-            send_b[group, 2 * k, member] = weighted(2 * k, done)
-        turned = []
-        for a, (vr, vi) in enumerate(values):
-            c, s = math.cos(TAU * a / devices), -math.sin(TAU * a / devices)
-            cs, ss = sign * c, sign * s
-            turned.append((vr * cs, vi * cs) if a == 0 else (vr * cs - vi * ss, vr * ss + vi * cs))
-        for k, done in enumerate(real_transform(turned)):
-            send_b[group, 2 * k + 1, member] = weighted(2 * k + 1, done)
+    lanes = lax.broadcasted_iota(jnp.int32, (tall, LANES), 1)
+    lines = lax.broadcasted_iota(jnp.int32, (tall, LANES), 0)
+    base = plane.astype(jnp.float32) * 0.25 - 0.5
+
+    def finish(group, gather):
+        def body(member, at, first):
+            slot = ((lines + (place * depth + first)) * LANES + lanes) * GAP
+            within = (slot + (group * per + member)).astype(jnp.float32) / length
+            for kk in range(quarter):
+                centred = (base + kk / devices) + within
+                weight = jnp.exp(RATE * centred * centred) * length**-0.5
+                total[group, kk, member, at] = gather(kk, member, at) * weight
+
+        tiles(body)
 
     def edges(end):
         row = 0 if end else depth - 1
         shift = 1 if end else -1
 
-        @pl.loop(0, devices)
-        def _(k):
+        @pl.loop(0, quarter)
+        def _(kk):
             for group in range(groups):
-                edge[k, group * per : (group + 1) * per] = send_b[group, k, :, row]
-
-        @pl.loop(0, devices)
-        def _(target):
-            inside = jnp.logical_and(target + shift >= 0, target + shift < devices)
+                edge[kk, group * per : (group + 1) * per] = total[group, kk, :, row]
+
+        @pl.loop(0, quarter)
+        def _(kk):
+            target = plane * quarter + kk - shift
+            inside = jnp.logical_and(target >= 0, target < devices)
 
             @pl.when(jnp.logical_and(inside, target != me))
             def _():
-                copy_edge(target, end, side_of).start()
+                copy_edge(kk, end).start()
 
     def edges_sent(end):
         shift = 1 if end else -1
 
-        @pl.loop(0, devices)
-        def _(target):
-            inside = jnp.logical_and(target + shift >= 0, target + shift < devices)
+        @pl.loop(0, quarter)
+        def _(kk):
+            target = plane * quarter + kk - shift
+            inside = jnp.logical_and(target >= 0, target < devices)
 
             @pl.when(jnp.logical_and(inside, target != me))
             def _():
-                copy_edge(target, end, side_of).wait_send()
-
-    @pl.loop(0, groups)
-    def _(group):
-        @pl.when(group + AHEAD < groups)
-        def _():
-            spectra(group + AHEAD)
-
-        whole(recv_a, group, sem_sa, sem_ra).wait_recv()
-
-        @pl.loop(0, per)
-        def _(member):
-            combine(group, member)
+                copy_edge(kk, end).wait_send()
+
+    def last_stage(group):
+        copy_far(group).wait_recv()
+
+        @pl.when(is_outer)
+        def _():
+            copy_near(group).wait_recv()
+            finish(
+                group,
+                lambda kk, member, at: own[group, plane * quarter + kk, member, at]
+                + (arrived[group, 1, kk, member, at] + arrived[group, 0, kk, member, at]),
+            )
+
+        @pl.when(is_inner)
+        def _():
+            finish(
+                group,
+                lambda kk, member, at: both[group, plane * quarter + kk, member, at] + arrived[group, 0, kk, member, at],
+            )
 
         @pl.when(group == groups - 1)
         def _():
             for end in range(2):
-                @pl.when(place == (0 if end else half - 1))
+                @pl.when(place == (0 if end else quarter - 1))
                 def _():
                     edges(end)
 
-        copy_b(group, far(0)).start()
-
-        @pl.loop(1, half)
+        @pl.loop(1, quarter)
         def _(step):
-            copy_b(group, far(step)).start()
-            copy_b(group, near(step)).start()
-
-            @pl.when(group + AHEAD < groups)
+            copy_b(group, beside(step)).start()
+
+        out_ref[group, place] = total[group, place]
+
+    stages = (first_stage, second_stage, third_stage, last_stage)
+
+    @pl.loop(0, groups + len(stages) - 1)
+    def _(turn):
+        for lag, stage in enumerate(stages):
+            @pl.when(jnp.logical_and(turn >= lag, turn < groups + lag))
             def _():
-                copy_a(group + AHEAD, near(step)).start()
-
-        out_ref[group, me] = send_b[group, me]
+                stage(turn - lag)
 
     for end in range(2):
-        sender = 0 if end else half - 1
+        sender = 0 if end else quarter - 1
         bound = devices - 1 if end else 0
-        shift = 1 if end else -1
 
         @pl.when(me == bound)
         def _():
             halo_ref[end] = jnp.zeros(halo_ref.shape[1:], jnp.float32)
 
-        @pl.when(me != bound)
-        def _():
-            for source_side in range(2):
-                source = source_side * half + sender
-
-                @pl.when(me == source)
-                def _():
-                    halo_ref[end, source_side] = edge[me + shift]
-
-                @pl.when(me != source)
-                def _():
-                    copy_edge(me, end, source_side).wait_recv()
+        @pl.when(jnp.logical_and(me != bound, place == sender))
+        def _():
+            halo_ref[end] = edge[sender + (1 if end else -1)]
+
+        @pl.when(jnp.logical_and(me != bound, place != sender))
+        def _():
+            copy_edge(0, end).wait_recv()
 
     @pl.loop(0, groups)
     def _(group):
         whole(out_ref, group, sem_sb, sem_rb).wait_recv()
 
     for end in range(2):
-        @pl.when(place == (0 if end else half - 1))
+        @pl.when(place == (0 if end else quarter - 1))
         def _():
             edges_sent(end)
 
     @pl.loop(0, groups)
     def _(group):
         whole(send_a, group, sem_sa, sem_ra).wait_send()
-        whole(send_b, group, sem_sb, sem_rb).wait_send()
+        whole(total, group, sem_sb, sem_rb).wait_send()
+
+        @pl.when(is_outer)
+        def _():
+            copy_raw(group).wait_send()
+
+        @pl.when(is_inner)
+        def _():
+            copy_far(group).wait_send()
+            copy_far_outer(group).wait_send()
+            copy_near(group).wait_send()
 
 
 def across(samples, inner, outer):
@@ -375,8 +457,8 @@
     seg = samples.shape[2]
     length = seg * devices
     me = lax.axis_index("inner") * outer + lax.axis_index("outer")
-    half = devices // 2
-    depth = STEPS // half
+    quarter = devices // 4
+    depth = STEPS // quarter
     per = RADIX // GROUPS
     x = samples.reshape(2, RADIX, STEPS, LANES)
 
@@ -396,13 +478,14 @@
         [jnp.concatenate([cosine, -sine], axis=1), jnp.concatenate([sine, cosine], axis=1)], axis=0
     )
     vmem = pl.BlockSpec(memory_space=pltpu.VMEM)
-    first = (GROUPS, half, 2, per, depth, LANES)
-    block = (GROUPS, devices, per, depth, LANES)
+    first = (GROUPS, quarter, 2, per, depth, LANES)
+    block = (GROUPS, quarter, per, depth, LANES)
+    wide = (GROUPS, devices, per, depth, LANES)
     return pl.pallas_call(
         functools.partial(across_kernel, inner, outer),
         out_shape=(
             jax.ShapeDtypeStruct(block, jnp.float32),
-            jax.ShapeDtypeStruct((2, 2, RADIX, LANES), jnp.float32),
+            jax.ShapeDtypeStruct((2, RADIX, LANES), jnp.float32),
         ),
         in_specs=[pl.BlockSpec(memory_space=pltpu.HBM)] * 2 + [vmem] * 3,
         out_specs=(vmem, vmem),
@@ -413,12 +496,18 @@
             pltpu.VMEM((2, STEPS, LANES), jnp.float32),
             pltpu.VMEM(first, jnp.float32),
             pltpu.VMEM(first, jnp.float32),
+            pltpu.VMEM(first, jnp.float32),
+            pltpu.VMEM(wide, jnp.float32),
+            pltpu.VMEM(wide, jnp.float32),
+            pltpu.VMEM((GROUPS, 2, quarter, per, depth, LANES), jnp.float32),
             pltpu.VMEM(block, jnp.float32),
-            pltpu.VMEM((devices, RADIX, LANES), jnp.float32),
+            pltpu.VMEM((quarter, RADIX, LANES), jnp.float32),
         ]
         + [pltpu.SemaphoreType.DMA((2,)), pltpu.SemaphoreType.DMA((RADIX,))]
         + [pltpu.SemaphoreType.DMA((GROUPS,))] * 4
-        + [pltpu.SemaphoreType.DMA((devices,)), pltpu.SemaphoreType.DMA((2, 2))],
+        + [pltpu.SemaphoreType.DMA((GROUPS, 3)), pltpu.SemaphoreType.DMA((GROUPS, 2))]
+        + [pltpu.SemaphoreType.DMA((GROUPS,))] * 2
+        + [pltpu.SemaphoreType.DMA((quarter,)), pltpu.SemaphoreType.DMA((2,))],
         compiler_params=pltpu.CompilerParams(
             collective_id=0, has_side_effects=True, vmem_limit_bytes=48 * 2**20
         ),
@@ -428,18 +517,15 @@
 def gram_kernel(inner, outer, real_ref, halo_ref, index_ref, offset_ref, weight_ref, order_ref, z_ref, gram_ref, field):
     devices = inner * outer
     groups, _, per, depth, _ = real_ref.shape
-    half = devices // 2
-
-    @pl.loop(0, half)
+
+    @pl.loop(0, devices // 4)
     def _(e):
         at = pl.ds(pl.multiple_of(8 + e * depth, math.gcd(8, depth)), depth)
         for group in range(groups):
-            members = slice(group * per, (group + 1) * per)
-            field[members, at, :] = real_ref[group, e] + real_ref[group, half + e]
-
-    halo = halo_ref[:, 0] + halo_ref[:, 1]
-    field[:, 7:8, :] = halo[0][:, None, :]
-    field[:, STEPS + 8 : STEPS + 9, :] = halo[1][:, None, :]
+            field[group * per : (group + 1) * per, at, :] = real_ref[group, e]
+
+    field[:, 7:8, :] = halo_ref[0][:, None, :]
+    field[:, STEPS + 8 : STEPS + 9, :] = halo_ref[1][:, None, :]
 
     lane = lax.broadcasted_iota(jnp.int32, (8, LANES), 1)
 

time: 77.3 us -> 81.2 us (1.050)
  Pallas kernels: 74 us -> 77.8 us
    pallas_call x1, Pallas kernels: 68.3 us -> 72.2 us  [across(): pl.pallas_call(functools.partial(across_kernel, inner, outer), out_shape=...]
where the time goes in v4:
time: 81.2 us; the launch traced here: 81 us
  Pallas kernels  77.8 us (96%)
  local copies, waits for them, and re-layouts  1.61 us (2%)
  other arithmetic  0.85 us (1%)
    pallas_call x1, Pallas kernels, across(): pl.pallas_call(functools.partial(across_kernel, inner, outer), out_shape=...  72.2 us
    pallas_call x1, Pallas kernels, local(): pl.pallas_call(functools.partial(gram_kernel, inner, outer), out_shape=(j...  5.64 us

profile of v4, /device:TPU:0, one launch (start us, length us, event | category | flops | bytes accessed | tf_op | source)
XLA Modules:
  0.0 81.0 jit_solution(7903526459563716311)
XLA Ops:
  0.6 0.0 copy-start.3
  0.6 0.0 copy-start.4
  0.7 0.0 copy-start.2
  0.7 0.0 copy-start.1
  0.7 0.3 fusion.10
  1.1 0.5 fusion.1
  1.6 0.0 copy-start
  1.6 1.6 %copy-done = f32[2,1,262144]{2,1,0:T(1,128)S(1)} copy-done((f32[2,1,262144]{2,1,0:T(1,128)S(1)}, f32[2,1,262144]{2,1,0:T(1,128)}, u32[]{:S(2)}) %copy-start) | copy-done | bytes 2097176
  3.2 72.2 %shard_map.77 = (f32[8,8,1,32,128]{4,3,2,1,0:T(8,128)S(1)}, f32[2,8,128]{2,1,0:T(8,128)S(1)}) custom-call(f32[2,8,256,128]{3,2,1,0:T(8,128)S(1)} %bitcast.5, bf16[8,4,256,256]{3,2,1,0:T(8,128)(2,1)} %constant.41.clone.stage_hbm, f32[2,256,128]{2,1,0:T(8,128)S(1)} %pad_maximum_fusion.u_ref, f32[2,8,128]{2,1,0:T(8,128)S(1)} %pad_maximum_fusion.1.v_ref, ...), custom_call_target="tpu_custom_call" | custom-call | tf_op jit(solution)/shard_map/pallas_call | solution.py:484
  75.3 0.0 copy-done.3
  75.4 0.0 copy-done.4
  75.4 0.0 copy-done.2
  75.4 0.0 copy-done.1
  75.4 5.6 %shard_map.78 = (f32[2048,128]{1,0:T(8,128)}, f32[256,128]{1,0:T(8,128)}) custom-call(f32[8,8,1,32,128]{4,3,2,1,0:T(8,128)S(1)} %get-tuple-element.6.real_ref, f32[2,8,128]{2,1,0:T(8,128)S(1)} %get-tuple-element.7.halo_ref, s32[256,128]{1,0:T(8,128)S(1)} %bitcast.6, s32[256,128]{1,0:T(8,128)S(1)} %bitcast.7, f32[32,8,128]{2,1,0:T(8,128)S(1)} %copy-done.4, ...), custom_call_target="tpu_custom_call" | custom-call | tf_op jit(solution)/shard_map/pallas_call | solution.py:589
  (5 shorter events, 0.1 us)
Async XLA Ops:
  0.6 74.7 %copy-start.3 = (bf16[256,256]{1,0:T(8,128)(2,1)S(1)}, bf16[256,256]{1,0:T(8,128)(2,1)}, u32[]{:S(2)}) copy-start(bf16[256,256]{1,0:T(8,128)(2,1)} %constant.43.clone.order_ref) | copy-start | bytes 393220
  0.6 74.7 %copy-start.4 = (f32[32,8,128]{2,1,0:T(8,128)S(1)}, f32[32,8,128]{2,1,0:T(8,128)}, u32[]{:S(2)}) copy-start(f32[32,8,128]{2,1,0:T(8,128)} %constant.42.clone.weight_ref) | copy-start | bytes 393220
  0.7 74.7 %copy-start.2 = (s32[32768]{0:T(1024)S(1)}, s32[32768]{0:T(1024)}, u32[]{:S(2)}) copy-start(s32[32768]{0:T(1024)} %param.8) | copy-start | bytes 393220
  0.7 74.7 %copy-start.1 = (s32[32768]{0:T(1024)S(1)}, s32[32768]{0:T(1024)}, u32[]{:S(2)}) copy-start(s32[32768]{0:T(1024)} %param.7) | copy-start | bytes 393220
  1.6 1.6 %copy-start = (f32[2,1,262144]{2,1,0:T(1,128)S(1)}, f32[2,1,262144]{2,1,0:T(1,128)}, u32[]{:S(2)}) copy-start(f32[2,1,262144]{2,1,0:T(1,128)} %param.6) | copy-start | bytes 6291460

commit v5 on v4

--- a/solution.py
+++ b/solution.py
@@ -15,7 +15,8 @@
 LANES = 128
 RADIX = 8
 STEPS = 256
-GROUPS = 8
+SPLIT = 2
+GROUPS = RADIX * SPLIT
 TAU = 2.0 * math.pi
 RATE = 4.0
 MESH = pl.DeviceIdType.MESH
@@ -222,8 +223,7 @@
 
     last_high, last_low = halves(last_ref[...])
 
-    def spectrum(group, member):
-        p = group * per + member
+    def spectrum(p):
         load_table(p).wait()
         high, low = halves(parts[p])
         cos_high, cos_low, sin_high, sin_low = (stage_ref[p, i] for i in range(4))
@@ -241,12 +241,14 @@
             block = z[part * LANES : (part + 1) * LANES]
             for lane_half in range(2):
                 rows[part, pl.ds(lane_half, LANES, stride=2), :] = block[:, lane_half * LANES : (lane_half + 1) * LANES]
-            send_a[group, :, part, member] = rows[part].reshape(quarter, depth, LANES)
+            value = rows[part].reshape(quarter, SPLIT, depth, LANES)
+            for share in range(SPLIT):
+                send_a[p * SPLIT + share, :, part, 0] = value[:, share]
 
     def spectra(group):
-        @pl.loop(0, per)
-        def _(member):
-            spectrum(group, member)
+        @pl.when(group % SPLIT == 0)
+        def _():
+            spectrum(group // SPLIT)
 
         recv_a[group, place] = send_a[group, place]
 
@@ -331,8 +333,9 @@
 
     def finish(group, gather):
         def body(member, at, first):
-            slot = ((lines + (place * depth + first)) * LANES + lanes) * GAP
-            within = (slot + (group * per + member)).astype(jnp.float32) / length
+            row = (place * SPLIT + group % SPLIT) * depth + first
+            slot = ((lines + row) * LANES + lanes) * GAP
+            within = (slot + group // SPLIT).astype(jnp.float32) / length
             for kk in range(quarter):
                 centred = (base + kk / devices) + within
                 weight = jnp.exp(RATE * centred * centred) * length**-0.5
@@ -346,8 +349,8 @@
 
         @pl.loop(0, quarter)
         def _(kk):
-            for group in range(groups):
-                edge[kk, group * per : (group + 1) * per] = total[group, kk, :, row]
+            for p in range(RADIX):
+                edge[kk, p : p + 1] = total[p * SPLIT + (0 if end else SPLIT - 1), kk, :, row]
 
         @pl.loop(0, quarter)
         def _(kk):
@@ -402,11 +405,11 @@
 
         out_ref[group, place] = total[group, place]
 
-    stages = (first_stage, second_stage, third_stage, last_stage)
-
-    @pl.loop(0, groups + len(stages) - 1)
+    stages = ((0, first_stage), (1, second_stage), (3, third_stage), (5, last_stage))
+
+    @pl.loop(0, groups + 5)
     def _(turn):
-        for lag, stage in enumerate(stages):
+        for lag, stage in stages:
             @pl.when(jnp.logical_and(turn >= lag, turn < groups + lag))
             def _():
                 stage(turn - lag)
@@ -458,8 +461,8 @@
     length = seg * devices
     me = lax.axis_index("inner") * outer + lax.axis_index("outer")
     quarter = devices // 4
-    depth = STEPS // quarter
-    per = RADIX // GROUPS
+    depth = STEPS // (quarter * SPLIT)
+    per = 1
     x = samples.reshape(2, RADIX, STEPS, LANES)
 
     def phase(number, order):
@@ -520,9 +523,10 @@
 
     @pl.loop(0, devices // 4)
     def _(e):
-        at = pl.ds(pl.multiple_of(8 + e * depth, math.gcd(8, depth)), depth)
-        for group in range(groups):
-            field[group * per : (group + 1) * per, at, :] = real_ref[group, e]
+        for share in range(SPLIT):
+            at = pl.ds(pl.multiple_of(8 + (e * SPLIT + share) * depth, math.gcd(8, depth)), depth)
+            for p in range(GAP):
+                field[p, at, :] = real_ref[p * SPLIT + share, e, 0]
 
     field[:, 7:8, :] = halo_ref[0][:, None, :]
     field[:, STEPS + 8 : STEPS + 9, :] = halo_ref[1][:, None, :]

time: 81.2 us -> 77.4 us (0.953)
  Pallas kernels: 77.8 us -> 74 us
    pallas_call x1, Pallas kernels: 72.2 us -> 68.4 us  [across(): pl.pallas_call(functools.partial(across_kernel, inner, outer), out_shape=...]
where the time goes in v5:
time: 77.4 us; the launch traced here: 77.2 us
  Pallas kernels  74 us (96%)
  local copies, waits for them, and re-layouts  1.61 us (2%)
  other arithmetic  0.85 us (1%)
    pallas_call x1, Pallas kernels, across(): pl.pallas_call(functools.partial(across_kernel, inner, outer), out_shape=...  68.4 us
    pallas_call x1, Pallas kernels, local(): pl.pallas_call(functools.partial(gram_kernel, inner, outer), out_shape=(j...  5.64 us
    unnamed x10, local copies, waits for them, and re-layouts  1.61 us

profile of v5, /device:TPU:0, one launch (start us, length us, event | category | flops | bytes accessed | tf_op | source)
XLA Modules:
  0.0 77.2 jit_solution(14751295277004173185)
XLA Ops:
  0.6 0.0 copy-start.3
  0.6 0.0 copy-start.4
  0.7 0.0 copy-start.2
  0.7 0.0 copy-start.1
  0.7 0.3 fusion.10
  1.1 0.5 fusion.1
  1.6 0.0 copy-start
  1.6 1.6 %copy-done = f32[2,1,262144]{2,1,0:T(1,128)S(1)} copy-done((f32[2,1,262144]{2,1,0:T(1,128)S(1)}, f32[2,1,262144]{2,1,0:T(1,128)}, u32[]{:S(2)}) %copy-start) | copy-done | bytes 2097176
  3.2 68.4 %shard_map.77 = (f32[16,8,1,16,128]{4,3,2,1,0:T(8,128)S(1)}, f32[2,8,128]{2,1,0:T(8,128)S(1)}) custom-call(f32[2,8,256,128]{3,2,1,0:T(8,128)S(1)} %bitcast.5, bf16[8,4,256,256]{3,2,1,0:T(8,128)(2,1)} %constant.41.clone.stage_hbm, f32[2,256,128]{2,1,0:T(8,128)S(1)} %pad_maximum_fusion.u_ref, f32[2,8,128]{2,1,0:T(8,128)S(1)} %pad_maximum_fusion.1.v_ref, ...), custom_call_target="tpu_custom_call" | custom-call | tf_op jit(solution)/shard_map/pallas_call | solution.py:487
  71.5 0.0 copy-done.3
  71.5 0.0 copy-done.4
  71.6 0.0 copy-done.2
  71.6 0.0 copy-done.1
  71.6 5.6 %shard_map.78 = (f32[2048,128]{1,0:T(8,128)}, f32[256,128]{1,0:T(8,128)}) custom-call(f32[16,8,1,16,128]{4,3,2,1,0:T(8,128)S(1)} %get-tuple-element.6.real_ref, f32[2,8,128]{2,1,0:T(8,128)S(1)} %get-tuple-element.7.halo_ref, s32[256,128]{1,0:T(8,128)S(1)} %bitcast.6, s32[256,128]{1,0:T(8,128)S(1)} %bitcast.7, f32[32,8,128]{2,1,0:T(8,128)S(1)} %copy-done.4, ...), custom_call_target="tpu_custom_call" | custom-call | tf_op jit(solution)/shard_map/pallas_call | solution.py:593
  (5 shorter events, 0.1 us)
Async XLA Ops:
  0.6 70.9 %copy-start.3 = (bf16[256,256]{1,0:T(8,128)(2,1)S(1)}, bf16[256,256]{1,0:T(8,128)(2,1)}, u32[]{:S(2)}) copy-start(bf16[256,256]{1,0:T(8,128)(2,1)} %constant.43.clone.order_ref) | copy-start | bytes 393220
  0.6 70.9 %copy-start.4 = (f32[32,8,128]{2,1,0:T(8,128)S(1)}, f32[32,8,128]{2,1,0:T(8,128)}, u32[]{:S(2)}) copy-start(f32[32,8,128]{2,1,0:T(8,128)} %constant.42.clone.weight_ref) | copy-start | bytes 393220
  0.7 70.9 %copy-start.2 = (s32[32768]{0:T(1024)S(1)}, s32[32768]{0:T(1024)}, u32[]{:S(2)}) copy-start(s32[32768]{0:T(1024)} %param.8) | copy-start | bytes 393220
  0.7 70.9 %copy-start.1 = (s32[32768]{0:T(1024)S(1)}, s32[32768]{0:T(1024)}, u32[]{:S(2)}) copy-start(s32[32768]{0:T(1024)} %param.7) | copy-start | bytes 393220
  1.6 1.6 %copy-start = (f32[2,1,262144]{2,1,0:T(1,128)S(1)}, f32[2,1,262144]{2,1,0:T(1,128)}, u32[]{:S(2)}) copy-start(f32[2,1,262144]{2,1,0:T(1,128)} %param.6) | copy-start | bytes 6291460

commit v6 on v5

--- a/solution.py
+++ b/solution.py
@@ -15,7 +15,7 @@
 LANES = 128
 RADIX = 8
 STEPS = 256
-SPLIT = 2
+SPLIT = 4
 GROUPS = RADIX * SPLIT
 TAU = 2.0 * math.pi
 RATE = 4.0
@@ -323,8 +323,8 @@
                     both[group, k, member, at] = done + own[group, k, member, at]
 
             tiles(body)
+            copy_far_outer(group).start()
             copy_far(group).start()
-            copy_far_outer(group).start()
 
     length = STEPS * LANES * GAP * devices
     lanes = lax.broadcasted_iota(jnp.int32, (tall, LANES), 1)
@@ -405,9 +405,9 @@
 
         out_ref[group, place] = total[group, place]
 
-    stages = ((0, first_stage), (1, second_stage), (3, third_stage), (5, last_stage))
-
-    @pl.loop(0, groups + 5)
+    stages = ((0, first_stage), (2, second_stage), (5, third_stage), (9, last_stage))
+
+    @pl.loop(0, groups + 9)
     def _(turn):
         for lag, stage in stages:
             @pl.when(jnp.logical_and(turn >= lag, turn < groups + lag))

time: 77.4 us -> 76.8 us (level)
  no operation moved by 1% of the time
where the time goes in v6:
time: 76.8 us; the launch traced here: 76.7 us
  Pallas kernels  73.4 us (96%)
  local copies, waits for them, and re-layouts  1.61 us (2%)
  other arithmetic  0.85 us (1%)
    pallas_call x1, Pallas kernels, across(): pl.pallas_call(functools.partial(across_kernel, inner, outer), out_shape=...  67.7 us
    pallas_call x1, Pallas kernels, local(): pl.pallas_call(functools.partial(gram_kernel, inner, outer), out_shape=(j...  5.71 us
    unnamed x10, local copies, waits for them, and re-layouts  1.61 us

profile of v6, /device:TPU:0, one launch (start us, length us, event | category | flops | bytes accessed | tf_op | source)
XLA Modules:
  0.0 76.7 jit_solution(10111203600226245527)
XLA Ops:
  0.6 0.0 copy-start.3
  0.6 0.0 copy-start.4
  0.7 0.0 copy-start.2
  0.7 0.0 copy-start.1
  0.7 0.3 fusion.10
  1.1 0.5 fusion.1
  1.6 0.0 copy-start
  1.6 1.6 %copy-done = f32[2,1,262144]{2,1,0:T(1,128)S(1)} copy-done((f32[2,1,262144]{2,1,0:T(1,128)S(1)}, f32[2,1,262144]{2,1,0:T(1,128)}, u32[]{:S(2)}) %copy-start) | copy-done | bytes 2097176
  3.2 67.7 %shard_map.77 = (f32[32,8,1,8,128]{4,3,2,1,0:T(8,128)S(1)}, f32[2,8,128]{2,1,0:T(8,128)S(1)}) custom-call(f32[2,8,256,128]{3,2,1,0:T(8,128)S(1)} %bitcast.5, bf16[8,4,256,256]{3,2,1,0:T(8,128)(2,1)} %constant.41.clone.stage_hbm, f32[2,256,128]{2,1,0:T(8,128)S(1)} %pad_maximum_fusion.u_ref, f32[2,8,128]{2,1,0:T(8,128)S(1)} %pad_maximum_fusion.1.v_ref, ...), custom_call_target="tpu_custom_call" | custom-call | tf_op jit(solution)/shard_map/pallas_call | solution.py:487
  70.9 0.0 copy-done.3
  70.9 0.0 copy-done.4
  70.9 0.0 copy-done.2
  70.9 0.0 copy-done.1
  71.0 5.7 %shard_map.78 = (f32[2048,128]{1,0:T(8,128)}, f32[256,128]{1,0:T(8,128)}) custom-call(f32[32,8,1,8,128]{4,3,2,1,0:T(8,128)S(1)} %get-tuple-element.6.real_ref, f32[2,8,128]{2,1,0:T(8,128)S(1)} %get-tuple-element.7.halo_ref, s32[256,128]{1,0:T(8,128)S(1)} %bitcast.6, s32[256,128]{1,0:T(8,128)S(1)} %bitcast.7, f32[32,8,128]{2,1,0:T(8,128)S(1)} %copy-done.4, ...), custom_call_target="tpu_custom_call" | custom-call | tf_op jit(solution)/shard_map/pallas_call | solution.py:593
  (5 shorter events, 0.1 us)
Async XLA Ops:
  0.6 70.3 %copy-start.3 = (bf16[256,256]{1,0:T(8,128)(2,1)S(1)}, bf16[256,256]{1,0:T(8,128)(2,1)}, u32[]{:S(2)}) copy-start(bf16[256,256]{1,0:T(8,128)(2,1)} %constant.43.clone.order_ref) | copy-start | bytes 393220
  0.6 70.3 %copy-start.4 = (f32[32,8,128]{2,1,0:T(8,128)S(1)}, f32[32,8,128]{2,1,0:T(8,128)}, u32[]{:S(2)}) copy-start(f32[32,8,128]{2,1,0:T(8,128)} %constant.42.clone.weight_ref) | copy-start | bytes 393220
  0.7 70.3 %copy-start.2 = (s32[32768]{0:T(1024)S(1)}, s32[32768]{0:T(1024)}, u32[]{:S(2)}) copy-start(s32[32768]{0:T(1024)} %param.8) | copy-start | bytes 393220
  0.7 70.3 %copy-start.1 = (s32[32768]{0:T(1024)S(1)}, s32[32768]{0:T(1024)}, u32[]{:S(2)}) copy-start(s32[32768]{0:T(1024)} %param.7) | copy-start | bytes 393220
  1.6 1.6 %copy-start = (f32[2,1,262144]{2,1,0:T(1,128)S(1)}, f32[2,1,262144]{2,1,0:T(1,128)}, u32[]{:S(2)}) copy-start(f32[2,1,262144]{2,1,0:T(1,128)} %param.6) | copy-start | bytes 6291460

commit v7 on v6

--- a/solution.py
+++ b/solution.py
@@ -15,7 +15,7 @@
 LANES = 128
 RADIX = 8
 STEPS = 256
-SPLIT = 4
+SPLIT = 2
 GROUPS = RADIX * SPLIT
 TAU = 2.0 * math.pi
 RATE = 4.0
@@ -405,9 +405,9 @@
 
         out_ref[group, place] = total[group, place]
 
-    stages = ((0, first_stage), (2, second_stage), (5, third_stage), (9, last_stage))
-
-    @pl.loop(0, groups + 9)
+    stages = ((0, first_stage), (1, second_stage), (3, third_stage), (6, last_stage))
+
+    @pl.loop(0, groups + 6)
     def _(turn):
         for lag, stage in stages:
             @pl.when(jnp.logical_and(turn >= lag, turn < groups + lag))
@@ -517,7 +517,7 @@
     )(x, jnp.asarray(stage_table()), u, v, last)
 
 
-def gram_kernel(inner, outer, real_ref, halo_ref, index_ref, offset_ref, weight_ref, order_ref, z_ref, gram_ref, field):
+def gram_kernel(inner, outer, real_ref, halo_ref, index_ref, offset_ref, weight_ref, order_ref, z_ref, gram_ref, field, ordered, sem):
     devices = inner * outer
     groups, _, per, depth, _ = real_ref.shape
 
@@ -530,6 +530,32 @@
 
     field[:, 7:8, :] = halo_ref[0][:, None, :]
     field[:, STEPS + 8 : STEPS + 9, :] = halo_ref[1][:, None, :]
+
+    width = 2 * LANES
+    share = width // GAP
+    run = lax.broadcasted_iota(jnp.int32, (STEPS, LANES), 1) // share
+    for column in range(LANES // share):
+        packed = []
+        for first in range(0, GAP, LANES // share):
+            piece = None
+            for place in range(LANES // share):
+                value = field[first + place, 8 : STEPS + 8, :]
+                turn = (place - column) * share % LANES
+                value = pltpu.roll(value, turn, 1) if turn else value
+                piece = value if piece is None else jnp.where(run == place, value, piece)
+            packed.append(piece)
+        rest = jnp.concatenate(packed, axis=1)
+        block = None
+        for _ in range(2):
+            piece = rest.astype(jnp.bfloat16)
+            rest = rest - piece.astype(jnp.float32)
+            product = jnp.dot(piece, order_ref[...], preferred_element_type=jnp.float32)
+            block = product if block is None else block + product
+        for side in range(2):
+            ordered[pl.ds(2 * column + side, STEPS, stride=GAP), :] = block[:, side * LANES : (side + 1) * LANES]
+
+    leave = pltpu.make_async_copy(ordered, z_ref, sem)
+    leave.start()
 
     lane = lax.broadcasted_iota(jnp.int32, (8, LANES), 1)
 
@@ -563,28 +589,7 @@
             total += window[tap] * jnp.take_along_axis(weight_ref[tap], offset, axis=1)
         gram_ref[pl.ds(row, 8)] = total
 
-    width = 2 * LANES
-    share = width // GAP
-    run = lax.broadcasted_iota(jnp.int32, (STEPS, LANES), 1) // share
-    for column in range(LANES // share):
-        packed = []
-        for first in range(0, GAP, LANES // share):
-            piece = None
-            for place in range(LANES // share):
-                value = field[first + place, 8 : STEPS + 8, :]
-                turn = (place - column) * share % LANES
-                value = pltpu.roll(value, turn, 1) if turn else value
-                piece = value if piece is None else jnp.where(run == place, value, piece)
-            packed.append(piece)
-        rest = jnp.concatenate(packed, axis=1)
-        block = None
-        for _ in range(3):
-            piece = rest.astype(jnp.bfloat16)
-            rest = rest - piece.astype(jnp.float32)
-            product = jnp.dot(piece, order_ref[...], preferred_element_type=jnp.float32)
-            block = product if block is None else block + product
-        for side in range(2):
-            z_ref[pl.ds(2 * column + side, STEPS, stride=GAP), :] = block[:, side * LANES : (side + 1) * LANES]
+    leave.wait()
 
 
 def local(inner, outer, samples, gram_index, gram_offset):
@@ -597,8 +602,12 @@
             jax.ShapeDtypeStruct(rows, jnp.float32),
         ),
         in_specs=[pl.BlockSpec(memory_space=pltpu.VMEM)] * 6,
-        out_specs=(pl.BlockSpec(memory_space=pltpu.VMEM),) * 2,
-        scratch_shapes=[pltpu.VMEM((GAP, STEPS + 16, LANES), jnp.float32)],
+        out_specs=(pl.BlockSpec(memory_space=pltpu.HBM), pl.BlockSpec(memory_space=pltpu.VMEM)),
+        scratch_shapes=[
+            pltpu.VMEM((GAP, STEPS + 16, LANES), jnp.float32),
+            pltpu.VMEM((STEPS * GAP, LANES), jnp.float32),
+            pltpu.SemaphoreType.DMA,
+        ],
         compiler_params=pltpu.CompilerParams(vmem_limit_bytes=48 * 2**20),
     )(
         real, halo, gram_index.reshape(rows), gram_offset.reshape(rows),

time: 76.8 us -> 76.1 us (level)
  no operation moved by 1% of the time
where the time goes in v7:
time: 76.1 us; the launch traced here: 76 us
  Pallas kernels  72.8 us (96%)
  local copies, waits for them, and re-layouts  1.61 us (2%)
  other arithmetic  0.85 us (1%)
    pallas_call x1, Pallas kernels, across(): pl.pallas_call(functools.partial(across_kernel, inner, outer), out_shape=...  67.5 us
    pallas_call x1, Pallas kernels, local(): pl.pallas_call(functools.partial(gram_kernel, inner, outer), out_shape=(j...  5.24 us
    unnamed x10, local copies, waits for them, and re-layouts  1.61 us

profile of v7, /device:TPU:0, one launch (start us, length us, event | category | flops | bytes accessed | tf_op | source)
XLA Modules:
  0.0 76.0 jit_solution(12097794061747494808)
XLA Ops:
  0.6 0.0 copy-start.3
  0.6 0.0 copy-start.4
  0.7 0.0 copy-start.2
  0.7 0.0 copy-start.1
  0.7 0.3 fusion.10
  1.1 0.5 fusion.1
  1.6 0.0 copy-start
  1.6 1.6 %copy-done = f32[2,1,262144]{2,1,0:T(1,128)S(1)} copy-done((f32[2,1,262144]{2,1,0:T(1,128)S(1)}, f32[2,1,262144]{2,1,0:T(1,128)}, u32[]{:S(2)}) %copy-start) | copy-done | bytes 2097176
  3.2 67.5 %shard_map.77 = (f32[16,8,1,16,128]{4,3,2,1,0:T(8,128)S(1)}, f32[2,8,128]{2,1,0:T(8,128)S(1)}) custom-call(f32[2,8,256,128]{3,2,1,0:T(8,128)S(1)} %bitcast.5, bf16[8,4,256,256]{3,2,1,0:T(8,128)(2,1)} %constant.41.clone.stage_hbm, f32[2,256,128]{2,1,0:T(8,128)S(1)} %pad_maximum_fusion.u_ref, f32[2,8,128]{2,1,0:T(8,128)S(1)} %pad_maximum_fusion.1.v_ref, ...), custom_call_target="tpu_custom_call" | custom-call | tf_op jit(solution)/shard_map/pallas_call | solution.py:487
  70.7 0.0 copy-done.3
  70.7 0.0 copy-done.4
  70.7 0.0 copy-done.2
  70.7 0.0 copy-done.1
  70.7 5.2 %shard_map.78 = (f32[2048,128]{1,0:T(8,128)}, f32[256,128]{1,0:T(8,128)}) custom-call(f32[16,8,1,16,128]{4,3,2,1,0:T(8,128)S(1)} %get-tuple-element.6.real_ref, f32[2,8,128]{2,1,0:T(8,128)S(1)} %get-tuple-element.7.halo_ref, s32[256,128]{1,0:T(8,128)S(1)} %bitcast.6, s32[256,128]{1,0:T(8,128)S(1)} %bitcast.7, f32[32,8,128]{2,1,0:T(8,128)S(1)} %copy-done.4, ...), custom_call_target="tpu_custom_call" | custom-call | tf_op jit(solution)/shard_map/pallas_call | solution.py:598
  (5 shorter events, 0.1 us)
Async XLA Ops:
  0.6 70.1 %copy-start.3 = (bf16[256,256]{1,0:T(8,128)(2,1)S(1)}, bf16[256,256]{1,0:T(8,128)(2,1)}, u32[]{:S(2)}) copy-start(bf16[256,256]{1,0:T(8,128)(2,1)} %constant.43.clone.order_ref) | copy-start | bytes 393220
  0.6 70.1 %copy-start.4 = (f32[32,8,128]{2,1,0:T(8,128)S(1)}, f32[32,8,128]{2,1,0:T(8,128)}, u32[]{:S(2)}) copy-start(f32[32,8,128]{2,1,0:T(8,128)} %constant.42.clone.weight_ref) | copy-start | bytes 393220
  0.7 70.1 %copy-start.2 = (s32[32768]{0:T(1024)S(1)}, s32[32768]{0:T(1024)}, u32[]{:S(2)}) copy-start(s32[32768]{0:T(1024)} %param.8) | copy-start | bytes 393220
  0.7 70.1 %copy-start.1 = (s32[32768]{0:T(1024)S(1)}, s32[32768]{0:T(1024)}, u32[]{:S(2)}) copy-start(s32[32768]{0:T(1024)} %param.7) | copy-start | bytes 393220
  1.6 1.6 %copy-start = (f32[2,1,262144]{2,1,0:T(1,128)S(1)}, f32[2,1,262144]{2,1,0:T(1,128)}, u32[]{:S(2)}) copy-start(f32[2,1,262144]{2,1,0:T(1,128)} %param.6) | copy-start | bytes 6291460

commit v8 on v7

--- a/solution.py
+++ b/solution.py
@@ -512,7 +512,7 @@
         + [pltpu.SemaphoreType.DMA((GROUPS,))] * 2
         + [pltpu.SemaphoreType.DMA((quarter,)), pltpu.SemaphoreType.DMA((2,))],
         compiler_params=pltpu.CompilerParams(
-            collective_id=0, has_side_effects=True, vmem_limit_bytes=48 * 2**20
+            collective_id=0, has_side_effects=True, vmem_limit_bytes=62 * 2**20
         ),
     )(x, jnp.asarray(stage_table()), u, v, last)
 

time: 76.1 us -> 80.3 us (1.055)
  other arithmetic: 0.85 us -> 2.86 us
  Pallas kernels: 72.8 us -> 74.6 us
    pallas_call x1, Pallas kernels: 67.5 us -> 69.3 us  [across(): pl.pallas_call(functools.partial(across_kernel, inner, outer), out_shape=...]
    unnamed x10 -> x12, local copies, waits for them, and re-layouts: 1.61 us -> 1.94 us
where the time goes in v8:
time: 80.3 us; the launch traced here: 80.1 us
  Pallas kernels  74.6 us (93%)
  other arithmetic  2.86 us (4%)
  local copies, waits for them, and re-layouts  1.94 us (2%)
    pallas_call x1, Pallas kernels, across(): pl.pallas_call(functools.partial(across_kernel, inner, outer), out_shape=...  69.3 us
    pallas_call x1, Pallas kernels, local(): pl.pallas_call(functools.partial(gram_kernel, inner, outer), out_shape=(j...  5.23 us
    unnamed x12, local copies, waits for them, and re-layouts  1.94 us

profile of v8, /device:TPU:0, one launch (start us, length us, event | category | flops | bytes accessed | tf_op | source)
XLA Modules:
  0.0 80.1 jit_solution(9689175153487033306)
XLA Ops:
  0.6 0.0 copy-start.3
  0.6 0.0 copy-start.4
  0.7 0.0 copy-start.2
  0.7 0.0 copy-start.1
  0.7 0.6 pad_maximum_fusion.1.v_ref
  1.3 0.3 fusion.10
  1.6 0.7 maximum_maximum_fusion.last_ref
  2.4 0.5 fusion.1
  2.8 0.7 pad_maximum_fusion.u_ref
  3.6 69.3 %shard_map.77 = (f32[16,8,1,16,128]{4,3,2,1,0:T(8,128)}, f32[2,8,128]{2,1,0:T(8,128)}) custom-call(f32[2,8,256,128]{3,2,1,0:T(8,128)} %bitcast.7, bf16[8,4,256,256]{3,2,1,0:T(8,128)(2,1)} %constant.41.clone.stage_hbm, f32[2,256,128]{2,1,0:T(8,128)} %pad_maximum_fusion.u_ref, f32[2,8,128]{2,1,0:T(8,128)} %pad_maximum_fusion.1.v_ref, ...), custom_call_target="tpu_custom_call" | custom-call | tf_op jit(solution)/shard_map/pallas_call | solution.py:487
  72.9 0.0 copy-done.3
  72.9 0.0 copy-done.4
  72.9 0.0 copy-done.2
  72.9 0.0 copy-done.1
  72.9 0.0 copy-start
  73.0 1.2 %copy-done = f32[16,8,1,16,128]{4,3,2,1,0:T(8,128)S(1)} copy-done((f32[16,8,1,16,128]{4,3,2,1,0:T(8,128)S(1)}, f32[16,8,1,16,128]{4,3,2,1,0:T(8,128)}, u32[]{:S(2)}) %copy-start) | copy-done | bytes 1048600
  74.2 0.0 copy-start.5
  74.2 0.7 copy-done.5
  74.9 5.2 %shard_map.78 = (f32[2048,128]{1,0:T(8,128)}, f32[256,128]{1,0:T(8,128)}) custom-call(f32[16,8,1,16,128]{4,3,2,1,0:T(8,128)S(1)} %copy-done, f32[2,8,128]{2,1,0:T(8,128)S(1)} %copy-done.5, s32[256,128]{1,0:T(8,128)S(1)} %bitcast.5, s32[256,128]{1,0:T(8,128)S(1)} %bitcast.6, f32[32,8,128]{2,1,0:T(8,128)S(1)} %copy-done.4, bf16[256,256]{1,0:T(8,128)(2,1)S(1)} %copy-done.3), custom_call_target="tpu_custom_call" | custom-call | tf_op jit(solution)/shard_map/pallas_call | solution.py:598
  (2 shorter events, 0.1 us)
Async XLA Ops:
  0.6 72.3 %copy-start.3 = (bf16[256,256]{1,0:T(8,128)(2,1)S(1)}, bf16[256,256]{1,0:T(8,128)(2,1)}, u32[]{:S(2)}) copy-start(bf16[256,256]{1,0:T(8,128)(2,1)} %constant.43.clone.order_ref) | copy-start | bytes 393220
  0.6 72.3 %copy-start.4 = (f32[32,8,128]{2,1,0:T(8,128)S(1)}, f32[32,8,128]{2,1,0:T(8,128)}, u32[]{:S(2)}) copy-start(f32[32,8,128]{2,1,0:T(8,128)} %constant.42.clone.weight_ref) | copy-start | bytes 393220
  0.7 72.3 %copy-start.2 = (s32[32768]{0:T(1024)S(1)}, s32[32768]{0:T(1024)}, u32[]{:S(2)}) copy-start(s32[32768]{0:T(1024)} %param.8) | copy-start | bytes 393220
  0.7 72.3 %copy-start.1 = (s32[32768]{0:T(1024)S(1)}, s32[32768]{0:T(1024)}, u32[]{:S(2)}) copy-start(s32[32768]{0:T(1024)} %param.7) | copy-start | bytes 393220
  72.9 1.2 %copy-start = (f32[16,8,1,16,128]{4,3,2,1,0:T(8,128)S(1)}, f32[16,8,1,16,128]{4,3,2,1,0:T(8,128)}, u32[]{:S(2)}) copy-start(f32[16,8,1,16,128]{4,3,2,1,0:T(8,128)} %get-tuple-element.6.real_ref) | copy-start | bytes 3145732
  74.2 0.7 copy-start.5
